TPU v7x, 32 devices: a whole 2x2x4 slice. The times are simulated.
32 devices in a mesh: dp: 8 (over z, x), head: 4 (over y, core).
Axes of the slice: x: 2, y: 2, z: 4, core: 2. Of those that a mesh axis runs over, the one named last changes fastest.
Arguments:
- layer_input: bfloat16 [512, 32, 768], P('head', 'dp'), may hold values from -6 to 6
- lengths: int32 [32], P('dp'), may hold values from 64 to 512, as said below
- cotangent: bfloat16 [512, 32, 768], P('head', 'dp'), may hold values from -6 to 6
- w_qkv: float32 [3, 768, 768], P(None, 'dp', 'head'), may hold values from -0.21875 to 0.21875
- w_out: float32 [768, 768], P('head', 'dp'), may hold values from -1.75 to 1.75
- w_up: float32 [768, 3072], P(None, ('dp', 'head')), may hold values from -0.21875 to 0.21875
- w_down: float32 [3072, 768], P(('dp', 'head')), may hold values from -0.109375 to 0.109375
- vectors: float32 [9216], P(('dp', 'head')), may hold values from -0.6 to 1.45
- mom_qkv: float32 [3, 768, 768], P(None, 'dp', 'head'), may hold values from -160 to 160
- mom_out: float32 [768, 768], P('head', 'dp'), may hold values from -80 to 80
- mom_up: float32 [768, 3072], P(None, ('dp', 'head')), may hold values from -80 to 80
- mom_down: float32 [3072, 768], P(('dp', 'head')), may hold values from -160 to 160
- mom_vec: float32 [9216], P(('dp', 'head')), may hold values from -384 to 384
- avg_qkv: float32 [3, 768, 768], P(None, 'dp', 'head'), may hold values from -0.21875 to 0.21875
- avg_out: float32 [768, 768], P('head', 'dp'), may hold values from -1.75 to 1.75
- avg_up: float32 [768, 3072], P(None, ('dp', 'head')), may hold values from -0.21875 to 0.21875
- avg_down: float32 [3072, 768], P(('dp', 'head')), may hold values from -0.109375 to 0.109375
- avg_vec: float32 [9216], P(('dp', 'head')), may hold values from -3 to 3
Outputs:
- layer_output: bfloat16 [512, 32, 768], P('head', 'dp')
- grad_input: float32 [512, 32, 768], P('head', 'dp')
- grad_qkv: float32 [3, 768, 768], P(None, 'dp', 'head')
- grad_out: float32 [768, 768], P('head', 'dp')
- grad_up: float32 [768, 3072], P(None, ('dp', 'head'))
- grad_down: float32 [3072, 768], P(('dp', 'head'))
- grad_vec: float32 [9216], P(('dp', 'head'))
- new_qkv: float32 [3, 768, 768], P(None, 'dp', 'head')
- new_out: float32 [768, 768], P('head', 'dp')
- new_up: float32 [768, 3072], P(None, ('dp', 'head'))
- new_down: float32 [3072, 768], P(('dp', 'head'))
- new_vec: float32 [9216], P(('dp', 'head'))
- new_mom_qkv: float32 [3, 768, 768], P(None, 'dp', 'head')
- new_mom_out: float32 [768, 768], P('head', 'dp')
- new_mom_up: float32 [768, 3072], P(None, ('dp', 'head'))
- new_mom_down: float32 [3072, 768], P(('dp', 'head'))
- new_mom_vec: float32 [9216], P(('dp', 'head'))
- new_avg_qkv: float32 [3, 768, 768], P(None, 'dp', 'head')
- new_avg_out: float32 [768, 768], P('head', 'dp')
- new_avg_up: float32 [768, 3072], P(None, ('dp', 'head'))
- new_avg_down: float32 [3072, 768], P(('dp', 'head'))
- new_avg_vec: float32 [9216], P(('dp', 'head'))
Inputs may be any that keep to these rules, and one draw needn't show every extreme that they name: `lengths`: in each aligned block of 2 documents at least one has length 512.
All inputs are finite; a program needn't handle non-finite values.
Results may differ from a plain program's by a relative error of at most 0.013.
The roundings to bfloat16 on the way count: a program that leaves them out, or rounds other values in their place, can miss the bound.
Values may be sent and summed in bfloat16 or wider, within the bound.
No kernel may reach another device: no remote copies, remote signals or barrier semaphores. Data moves between devices by JAX's collectives and lax.ppermute only.
A program may use at most 192 MiB of HBM per device.

v0:
```python
import math

import jax
import jax.numpy as jnp
from jax import lax
from jax.sharding import PartitionSpec as P

D = 768
HD = 64
FF = 3072
LEN = 512
MICRO = 2


EPSILON = 1e-05
MOMENTUM = 0.9
AVERAGE = 0.9
DECAY = 0.01
RATE_BASE = 0.05


def split_up(shard, dim, devices):
    lengths = shard.shape
    parts = shard.reshape(*lengths[:dim], devices, lengths[dim] // devices, *lengths[dim + 1 :])
    return jnp.moveaxis(parts, dim, 0)


def sent_and_summed(shard, axis, dim):
    devices = lax.axis_size(axis)
    parts = lax.all_to_all(split_up(shard, dim, devices), axis, 0, 0, tiled=True)
    return jnp.sum(parts.astype(jnp.float32), axis=0)


def norm_forward(values, gain, shift):
    center = values - jnp.mean(values, -1, keepdims=True)
    inverse = lax.rsqrt(jnp.mean(center * center, -1, keepdims=True) + EPSILON)
    normed = center * inverse
    return (normed * gain + shift, normed, inverse)


def norm_backward(d_result, normed, inverse, gain):
    d_normed = d_result * gain
    return inverse * (
        d_normed
        - jnp.mean(d_normed, -1, keepdims=True)
        - normed * jnp.mean(d_normed * normed, -1, keepdims=True)
    )


def gelu_slope(values):
    return (
        0.5 * (1.0 + lax.erf(values * 0.7071067811865476))
        + values * jnp.exp(-0.5 * values * values) * 0.3989422804014327
    )


def fetch_weights(w_qkv, w_out, w_up, w_down, vectors):
    attn_qkv, attn_out = (
        lax.all_gather(w_qkv.astype(jnp.bfloat16), "dp", axis=1, tiled=True),
        lax.all_gather(w_out.astype(jnp.bfloat16), "dp", axis=1, tiled=True),
    )
    ffn_up, ffn_down, small_vec = (
        lax.all_gather(w_up.astype(jnp.bfloat16), ("dp", "head"), axis=1, tiled=True),
        lax.all_gather(w_down.astype(jnp.bfloat16), ("dp", "head"), axis=0, tiled=True),
        lax.all_gather(vectors.astype(jnp.bfloat16), ("dp", "head"), axis=0, tiled=True),
    )
    return (attn_qkv, attn_out, ffn_up, ffn_down, small_vec)


def reduce_grads(grads):
    grad_qkv, grad_out, grad_up, grad_down, grad_vec = grads
    part_qkv, part_out = (
        sent_and_summed(grad_qkv.astype(jnp.bfloat16), "dp", 1),
        sent_and_summed(grad_out.astype(jnp.bfloat16), "dp", 1),
    )
    part_up, part_down, part_vec = (
        lax.psum_scatter(grad_up, ("dp", "head"), scatter_dimension=1, tiled=True),
        lax.psum_scatter(grad_down, ("dp", "head"), scatter_dimension=0, tiled=True),
        lax.psum_scatter(grad_vec, ("dp", "head"), scatter_dimension=0, tiled=True),
    )
    return (part_qkv, part_out, part_up, part_down, part_vec)


def masked_scores(queries, key_heads, allowed):
    raw_scores = jnp.einsum(
        "lbhe,mbhe->bhlm", queries, key_heads, preferred_element_type=jnp.float32
    ) * HD ** (-0.5)
    return jnp.where(allowed, raw_scores, -1e30)


def micro_pass(input_part, len_part, cot_part, weights):
    attn_qkv, attn_out, ffn_up, ffn_down, small_vec = weights
    vec_rows = small_vec.astype(jnp.float32).reshape(12, D)
    head_width = attn_qkv.shape[2]
    local_heads = head_width // HD
    head_rank = lax.axis_index("head")
    col_start = head_rank * head_width
    bias_q = lax.dynamic_slice_in_dim(vec_rows[0], col_start, head_width)
    bias_v = lax.dynamic_slice_in_dim(vec_rows[1], col_start, head_width)
    row_count = input_part.shape[0]
    gathered = lax.all_gather(input_part, "head", axis=0, tiled=True)
    length, batch = (gathered.shape[0], gathered.shape[1])
    projected = jnp.einsum("lbd,jde->jlbe", gathered, attn_qkv, preferred_element_type=jnp.float32)
    queries = (projected[0] + bias_q).astype(jnp.bfloat16).reshape(length, batch, local_heads, HD)
    key_heads = projected[1].astype(jnp.bfloat16).reshape(length, batch, local_heads, HD)
    value_heads = (
        (projected[2] + bias_v).astype(jnp.bfloat16).reshape(length, batch, local_heads, HD)
    )
    allowed = (jnp.arange(length)[None, :] < len_part[:, None])[:, None, None, :]
    scores = masked_scores(queries, key_heads, allowed)
    peak_score = jnp.max(scores, -1, keepdims=True)
    log_total = peak_score + jnp.log(jnp.sum(jnp.exp(scores - peak_score), -1, keepdims=True))
    probs_b = jnp.exp(scores - log_total).astype(jnp.bfloat16)
    context = jnp.einsum(
        "bhlm,mbhe->lbhe", probs_b, value_heads, preferred_element_type=jnp.float32
    )
    context = context.astype(jnp.bfloat16).reshape(length, batch, head_width)
    piece = context
    attn_mix = lax.psum_scatter(
        jnp.einsum("lbk,kd->lbd", piece, attn_out, preferred_element_type=jnp.float32),
        "head",
        scatter_dimension=0,
        tiled=True,
    )
    first_res = input_part.astype(jnp.float32) + attn_mix + vec_rows[2]
    hidden_one, normed_one, inverse_one = norm_forward(first_res, vec_rows[3], vec_rows[4])
    hidden_b = hidden_one.astype(jnp.bfloat16)
    up_pre = jnp.einsum(
        "lbd,df->lbf", hidden_b, ffn_up, preferred_element_type=jnp.float32
    ) + vec_rows[5:9].reshape(FF)
    act_b = jax.nn.gelu(up_pre, approximate=False).astype(jnp.bfloat16)
    second_res = hidden_one + (
        jnp.einsum("lbf,fd->lbd", act_b, ffn_down, preferred_element_type=jnp.float32) + vec_rows[9]
    )
    result, normed_two, inverse_two = norm_forward(second_res, vec_rows[10], vec_rows[11])
    position = head_rank * row_count + jnp.arange(row_count)
    alive = (position[:, None] < len_part[None, :])[:, :, None]
    d_result = jnp.where(alive, cot_part.astype(jnp.float32), 0.0)
    d_gain_two = jnp.sum(d_result * normed_two, (0, 1))
    d_shift_two = jnp.sum(d_result, (0, 1))
    d_second = norm_backward(d_result, normed_two, inverse_two, vec_rows[10])
    d_bias_down = jnp.sum(d_second, (0, 1))
    d_second_b = d_second.astype(jnp.bfloat16)
    grad_down = jnp.einsum("lbf,lbd->fd", act_b, d_second_b, preferred_element_type=jnp.float32)
    d_act = jnp.einsum("lbd,fd->lbf", d_second_b, ffn_down, preferred_element_type=jnp.float32)
    d_up = d_act * gelu_slope(up_pre)
    d_bias_up = jnp.sum(d_up, (0, 1))
    d_up_b = d_up.astype(jnp.bfloat16)
    grad_up = jnp.einsum("lbd,lbf->df", hidden_b, d_up_b, preferred_element_type=jnp.float32)
    d_hidden = d_second + jnp.einsum(
        "lbf,df->lbd", d_up_b, ffn_up, preferred_element_type=jnp.float32
    )
    d_gain_one = jnp.sum(d_hidden * normed_one, (0, 1))
    d_shift_one = jnp.sum(d_hidden, (0, 1))
    d_first = norm_backward(d_hidden, normed_one, inverse_one, vec_rows[3])
    d_bias_out = jnp.sum(d_first, (0, 1))
    d_first_b = d_first.astype(jnp.bfloat16)
    d_mix_all = lax.all_gather(d_first_b, "head", axis=0, tiled=True)
    grad_out = jnp.einsum("lbk,lbd->kd", context, d_mix_all, preferred_element_type=jnp.float32)
    d_context = jnp.einsum("lbd,kd->lbk", d_mix_all, attn_out, preferred_element_type=jnp.float32)
    d_context = d_context.astype(jnp.bfloat16).reshape(length, batch, local_heads, HD)
    recomputed = masked_scores(queries, key_heads, allowed)
    probs = jnp.exp(recomputed - log_total)
    d_probs = jnp.einsum(
        "lbhe,mbhe->bhlm", d_context, value_heads, preferred_element_type=jnp.float32
    )
    delta_rows = jnp.sum(probs * d_probs, -1, keepdims=True)
    d_scores = (probs * (d_probs - delta_rows) * HD ** (-0.5)).astype(jnp.bfloat16)
    d_queries = jnp.einsum(
        "bhlm,mbhe->lbhe", d_scores, key_heads, preferred_element_type=jnp.float32
    )
    d_keys = jnp.einsum("bhlm,lbhe->mbhe", d_scores, queries, preferred_element_type=jnp.float32)
    d_values = jnp.einsum(
        "bhlm,lbhe->mbhe", probs.astype(jnp.bfloat16), d_context, preferred_element_type=jnp.float32
    )
    d_queries = d_queries.reshape(length, batch, head_width)
    d_keys = d_keys.reshape(length, batch, head_width)
    d_values = d_values.reshape(length, batch, head_width)
    zeros_row = jnp.zeros((D,), jnp.float32)
    d_bias_q = lax.dynamic_update_slice_in_dim(zeros_row, jnp.sum(d_queries, (0, 1)), col_start, 0)
    d_bias_v = lax.dynamic_update_slice_in_dim(zeros_row, jnp.sum(d_values, (0, 1)), col_start, 0)
    d_proj = jnp.stack([d_queries, d_keys, d_values]).astype(jnp.bfloat16)
    grad_qkv = jnp.einsum("lbd,jlbe->jde", gathered, d_proj, preferred_element_type=jnp.float32)
    piece = d_proj
    d_input = d_first + lax.psum_scatter(
        jnp.einsum("jlbe,jde->lbd", piece, attn_qkv, preferred_element_type=jnp.float32).astype(
            jnp.bfloat16
        ),
        "head",
        scatter_dimension=0,
        tiled=True,
    ).astype(jnp.float32)
    grad_vec = jnp.concatenate(
        [
            d_bias_q,
            d_bias_v,
            d_bias_out,
            d_gain_one,
            d_shift_one,
            d_bias_up,
            d_bias_down,
            d_gain_two,
            d_shift_two,
        ]
    )
    return (
        result.astype(jnp.bfloat16),
        d_input,
        (grad_qkv, grad_out, grad_up, grad_down, grad_vec),
    )


def advance(weight, grad, moment, average, decay, rate):
    step_grad = grad + decay * weight
    moment_new = MOMENTUM * moment + step_grad
    weight_new = weight - rate * (step_grad + MOMENTUM * moment_new)
    average_new = AVERAGE * average + (1.0 - AVERAGE) * weight_new
    return (weight_new, moment_new, average_new)


def body(
    layer_input,
    lengths,
    cotangent,
    w_qkv,
    w_out,
    w_up,
    w_down,
    vectors,
    mom_qkv,
    mom_out,
    mom_up,
    mom_down,
    mom_vec,
    avg_qkv,
    avg_out,
    avg_up,
    avg_down,
    avg_vec,
):
    per_micro = layer_input.shape[1] // MICRO
    output_parts = []
    input_grads = []
    summed = None
    collected = None
    for micro_index in range(MICRO):
        current = fetch_weights(w_qkv, w_out, w_up, w_down, vectors)
        first_doc = micro_index * per_micro
        result_part, d_input_part, grads = micro_pass(
            layer_input[:, first_doc : first_doc + per_micro],
            lengths[first_doc : first_doc + per_micro],
            cotangent[:, first_doc : first_doc + per_micro],
            current,
        )
        output_parts.append(result_part)
        input_grads.append(d_input_part)
        collected = grads if collected is None else jax.tree.map(jnp.add, collected, grads)
    summed = reduce_grads(collected)
    grad_qkv, grad_out, grad_up, grad_down, grad_vec = summed
    total_slots = (
        layer_input.shape[0] * lax.axis_size("head") * layer_input.shape[1] * lax.axis_size("dp")
    )
    rate = RATE_BASE / math.sqrt(total_slots)
    rate_out = rate * math.sqrt(LEN / 8.0)
    new_qkv, new_mom_qkv, new_avg_qkv = advance(w_qkv, grad_qkv, mom_qkv, avg_qkv, DECAY, rate)
    new_out, new_mom_out, new_avg_out = advance(w_out, grad_out, mom_out, avg_out, DECAY, rate_out)
    new_up, new_mom_up, new_avg_up = advance(w_up, grad_up, mom_up, avg_up, DECAY, rate)
    new_down, new_mom_down, new_avg_down = advance(
        w_down, grad_down, mom_down, avg_down, DECAY, rate
    )
    new_vec, new_mom_vec, new_avg_vec = advance(vectors, grad_vec, mom_vec, avg_vec, 0.0, rate)
    return (
        jnp.concatenate(output_parts, 1),
        jnp.concatenate(input_grads, 1),
        grad_qkv,
        grad_out,
        grad_up,
        grad_down,
        grad_vec,
        new_qkv,
        new_out,
        new_up,
        new_down,
        new_vec,
        new_mom_qkv,
        new_mom_out,
        new_mom_up,
        new_mom_down,
        new_mom_vec,
        new_avg_qkv,
        new_avg_out,
        new_avg_up,
        new_avg_down,
        new_avg_vec,
    )


def solution(mesh):
    return jax.shard_map(
        body,
        mesh=mesh,
        in_specs=(
            P("head", "dp", None),
            P("dp"),
            P("head", "dp", None),
            P(None, "dp", "head"),
            P("head", "dp"),
            P(None, ("dp", "head")),
            P(("dp", "head"), None),
            P(("dp", "head")),
            P(None, "dp", "head"),
            P("head", "dp"),
            P(None, ("dp", "head")),
            P(("dp", "head"), None),
            P(("dp", "head")),
            P(None, "dp", "head"),
            P("head", "dp"),
            P(None, ("dp", "head")),
            P(("dp", "head"), None),
            P(("dp", "head")),
        ),
        out_specs=(
            P("head", "dp", None),
            P("head", "dp", None),
            P(None, "dp", "head"),
            P("head", "dp"),
            P(None, ("dp", "head")),
            P(("dp", "head"), None),
            P(("dp", "head")),
            P(None, "dp", "head"),
            P("head", "dp"),
            P(None, ("dp", "head")),
            P(("dp", "head"), None),
            P(("dp", "head")),
            P(None, "dp", "head"),
            P("head", "dp"),
            P(None, ("dp", "head")),
            P(("dp", "head"), None),
            P(("dp", "head")),
            P(None, "dp", "head"),
            P("head", "dp"),
            P(None, ("dp", "head")),
            P(("dp", "head"), None),
            P(("dp", "head")),
        ),
        check_vma=False,
    )
```

profile of v0, /device:TPU:0, one launch (start us, length us, event | category | flops | bytes accessed | tf_op | source)
XLA Modules:
  0.0 773.2 jit_solution(11042345418330769873)
XLA Ops:
  12.4 42.6 %all-reduce = bf16[9216]{0:T(1024)(128)(2,1)S(1)} all-reduce(bf16[9216]{0:T(1024)(128)(2,1)S(1)} %dynamic-update-slice), channel_id=1, replica_groups=mesh['dp'=8,'head'=4] {'dp','head'}, use_global_device_ids=true, to_apply=%add | all-reduce | flops 9216 | bytes 36864
  56.2 31.1 %all_gather.35 = bf16[192,768]{0,1:T(8,128)(2,1)S(1)} all-gather(bf16[192,96]{0,1:T(8,128)(2,1)S(1)} %copy.120), channel_id=1, replica_groups=mesh['dp'=8,'head'=4] {'dp'}, dimensions={1}, use_global_device_ids=true | all-gather | bytes 331776 | tf_op jit(solution)/shard_map/all_gather | solution.py:60
  87.3 38.0 %all_gather.32 = bf16[3,768,192]{2,0,1:T(4,128)(2,1)S(1)} all-gather(bf16[3,96,192]{2,0,1:T(4,128)(2,1)S(1)} %copy.117), channel_id=1, replica_groups=mesh['dp'=8,'head'=4] {'dp'}, dimensions={1}, use_global_device_ids=true | all-gather | bytes 995328 | tf_op jit(solution)/shard_map/all_gather | solution.py:59
  155.6 20.9 %reduce-scatter.7.cloned.1.call-done = f32[128,2,768]{2,0,1:T(8,128)} async-done(((f32[512,2,768]{2,0,1:T(8,128)}), f32[128,2,768]{2,0,1:T(8,128)}) %reduce-scatter.7.cloned.1.call-update) | async-done | bytes 786448 | tf_op jit(solution)/shard_map/reduce_scatter | solution.py:119
  176.4 40.8 %reduce-scatter.9.cloned.1.call-done = f32[128,2,768]{2,0,1:T(8,128)} async-done(((f32[512,2,768]{2,0,1:T(8,128)}), f32[128,2,768]{2,0,1:T(8,128)}) %reduce-scatter.9.cloned.1.call-update) | async-done | bytes 786448 | tf_op jit(solution)/shard_map/reduce_scatter | solution.py:119
  219.9 13.2 %all-gather.9.cloned.1.call-done = bf16[768,3072]{0,1:T(8,128)(2,1)} async-done(((bf16[768,96]{0,1:T(8,128)(2,1)}), bf16[768,3072]{0,1:T(8,128)(2,1)}) %all-gather.9.cloned.1.call-update) | async-done | bytes 4718608 | tf_op jit(solution)/shard_map/all_gather | solution.py:63
  233.1 4.5 fusion.143
  239.4 7.4 fusion.52
  246.9 52.2 %all-gather.11.cloned.1.call-done = bf16[3072,768]{1,0:T(8,128)(2,1)} async-done(((bf16[96,768]{1,0:T(8,128)(2,1)}), bf16[3072,768]{1,0:T(8,128)(2,1)}) %all-gather.11.cloned.1.call-update) | async-done | bytes 4718608 | tf_op jit(solution)/shard_map/all_gather | solution.py:64
  299.1 4.2 fusion.218
  304.2 4.2 fusion.224
  312.9 19.0 %fusion.55 = bf16[128,2,3072]{2,0,1:T(8,128)(2,1)S(1)} fusion(f32[128,2,3072]{2,0,1:T(8,128)S(1)} %get-tuple-element.180, u8[128,3072]{1,0:T(8,128)(4,1)S(1)} %get-tuple-element.91, u8[128,3072]{1,0:T(8,128)(4,1)S(1)} %get-tuple-element.90), kind=kLoop, calls=%fused_computation.51 | loop fusion | flops 55050240 | bytes 5505024 | tf_op jit(solution)/shard_map/convert_element_type | solution.py:131
  336.1 4.3 fusion.225
  340.4 3.5 fusion.205
  348.5 16.0 %all-gather.17.cloned.1.call-done = bf16[512,2,768]{2,0,1:T(8,128)(2,1)} async-done(((bf16[128,2,768]{2,0,1:T(8,128)(2,1)}), bf16[512,2,768]{2,0,1:T(8,128)(2,1)}) %all-gather.17.cloned.1.call-update) | async-done | bytes 1572880 | tf_op jit(solution)/shard_map/all_gather | solution.py:158
  367.4 4.9 fusion.160
  372.4 13.4 %fusion.211 = (f32[3,64]{1,0:T(4,128)}, bf16[512,2,3,64]{0,3,2,1:T(8,128)(2,1)}) fusion(bf16[512,2,3,64]{0,3,2,1:T(8,128)(2,1)} %bitcast.224, f32[2,3,512,512]{2,3,1,0:T(8,128)} %fusion.160, f32[2,3,512]{2,1,0:T(4,128)} %copy-done.95, f32[2,3,512,512]{2,3,1,0:T(8,128)} %copy-done.1, pred[2,512]{1,0:T(4,128)(4,1)} %copy-done.68), kind=kOutput, calls=%fused_computation.310 | convolution fusion | flops 219024704 | bytes 13383424 | tf_op jit(solution)/shard_map/bhlm,mbhe->lbhe/dot_general | solution.py:169
  385.8 12.9 %fusion.118 = bf16[2,3,64,512]{3,2,1,0:T(8,128)(2,1)} fusion(f32[2,3,512,512]{2,3,1,0:T(8,128)} %fusion.160, f32[2,3,512]{2,1,0:T(4,128)} %copy-done.95, f32[2,3,512,512]{2,3,1,0:T(8,128)} %copy-done.1, pred[2,512]{1,0:T(4,128)(4,1)} %copy-done.68, f32[512,2,3,64]{0,3,2,1:T(8,128)} %bitcast.216, f32[3,64]{1,0:T(4,128)S(1)} %add.306), kind=kOutput, calls=%fused_computation.128 | convolution fusion | flops 219221504 | bytes 13776640 | tf_op jit(solution)/shard_map/bhlm,lbhe->mbhe/dot_general | solution.py:172
  398.7 5.3 fusion.210
  410.7 5.0 fusion.158
  415.7 13.3 %fusion.213 = (f32[3,64]{1,0:T(4,128)}, bf16[512,2,3,64]{0,3,2,1:T(8,128)(2,1)}) fusion(bf16[512,2,3,64]{0,3,2,1:T(8,128)(2,1)S(1)} %bitcast.222, f32[2,3,512,512]{2,3,1,0:T(8,128)} %fusion.158, f32[2,3,512]{2,1,0:T(4,128)} %copy-done.94, f32[2,3,512,512]{2,3,1,0:T(8,128)} %copy-done, pred[2,512]{1,0:T(4,128)(4,1)} %copy-done.67), kind=kOutput, calls=%fused_computation.312 | convolution fusion | flops 219024704 | bytes 13383424 | tf_op jit(solution)/shard_map/bhlm,mbhe->lbhe/dot_general | solution.py:169
  429.0 13.0 %fusion.121 = bf16[2,3,64,512]{3,2,1,0:T(8,128)(2,1)} fusion(f32[2,3,512,512]{2,3,1,0:T(8,128)} %fusion.158, f32[2,3,512]{2,1,0:T(4,128)} %copy-done.94, f32[2,3,512,512]{2,3,1,0:T(8,128)} %copy-done, pred[2,512]{1,0:T(4,128)(4,1)} %copy-done.67, f32[512,2,3,64]{0,3,2,1:T(8,128)} %bitcast.214, f32[3,64]{1,0:T(4,128)S(1)} %add.306), kind=kOutput, calls=%fused_computation.129 | convolution fusion | flops 219221504 | bytes 13776640 | tf_op jit(solution)/shard_map/bhlm,lbhe->mbhe/dot_general | solution.py:172
  442.0 5.1 fusion.212
  450.9 3.3 fusion.155
  454.3 5.5 bitcast_add_fusion
  463.1 5.3 bitcast_add_fusion.1
  479.8 5.8 all-to-all-start.1
  493.2 4.4 all-to-all-done.1
  497.6 3.6 all-to-all-start
  514.8 42.5 %all-reduce.1 = f32[9216]{0:T(1024)S(1)} all-reduce(f32[9216]{0:T(1024)S(1)} %add.350), channel_id=8, replica_groups=mesh['dp'=8,'head'=4] {'dp','head'}, use_global_device_ids=true, to_apply=%region_48.49.clone | all-reduce | flops 9216 | bytes 73728
  570.4 51.1 %reduce-scatter.17.cloned.1.call-done = f32[96,768]{1,0:T(8,128)} async-done(((f32[3072,768]{1,0:T(8,128)}), f32[96,768]{1,0:T(8,128)}) %reduce-scatter.17.cloned.1.call-update) | async-done | bytes 294928 | tf_op jit(solution)/shard_map/reduce_scatter | solution.py:78
  623.4 140.1 %reduce-scatter.15.cloned.1.call-done = f32[768,96]{0,1:T(8,128)} async-done(((f32[768,3072]{0,1:T(8,128)}), f32[768,96]{0,1:T(8,128)}) %reduce-scatter.15.cloned.1.call-update) | async-done | bytes 294928 | tf_op jit(solution)/shard_map/reduce_scatter | solution.py:77
  (440 shorter events, 118.8 us)
Async XLA Ops:
  8.1 119.6 %all-gather.7.cloned.1.call-start = ((), (), s32[]{:S(2)}) async-start(), calls=%async_computation.8 | async-start | bytes 1966080 | tf_op jit(solution)/shard_map/all_gather | solution.py:101
  11.1 128.5 %all-gather.13.cloned.1.call-start = ((), (), s32[]{:S(2)}) async-start(), calls=%async_computation.12 | async-start | bytes 1966080 | tf_op jit(solution)/shard_map/all_gather | solution.py:101
  11.9 164.5 %reduce-scatter.7.cloned.1.call-start = ((), (), s32[]{:S(2)}) async-start(), calls=%async_computation.9 | async-start | bytes 3932160 | tf_op jit(solution)/shard_map/reduce_scatter | solution.py:119
  12.1 118.4 %copy-start.110 = (s32[2]{0:T(128)}, s32[2]{0:T(128)S(1)}, u32[]{:S(2)}) copy-start(s32[2]{0:T(128)S(1)} %get-tuple-element.170) | copy-start | bytes 28
  12.1 118.4 %copy-start.112 = (s32[2]{0:T(128)}, s32[2]{0:T(128)S(1)}, u32[]{:S(2)}) copy-start(s32[2]{0:T(128)S(1)} %get-tuple-element.171) | copy-start | bytes 28
  55.0 75.5 %copy-start.58 = (bf16[9216]{0:T(1024)(128)(2,1)}, bf16[9216]{0:T(1024)(128)(2,1)S(1)}, u32[]{:S(2)}) copy-start(bf16[9216]{0:T(1024)(128)(2,1)S(1)} %all-reduce) | copy-start | bytes 55300
  55.9 89.8 %copy-start.62 = (f32[3,64]{1,0:T(4,128)}, f32[3,64]{1,0:T(4,128)S(1)}, u32[]{:S(2)}) copy-start(f32[3,64]{1,0:T(4,128)S(1)} %add.303) | copy-start | bytes 2308
  139.3 78.0 %reduce-scatter.9.cloned.1.call-start = ((), (), s32[]{:S(2)}) async-start(), calls=%async_computation.13 | async-start | bytes 3932160 | tf_op jit(solution)/shard_map/reduce_scatter | solution.py:119
  151.3 81.9 %all-gather.9.cloned.1.call-start = ((), (), s32[]{:S(2)}) async-start(), calls=%async_computation.10 | async-start | bytes 4866048 | tf_op jit(solution)/shard_map/all_gather | solution.py:63
  152.0 147.0 %all-gather.11.cloned.1.call-start = ((), (), s32[]{:S(2)}) async-start(), calls=%async_computation.11 | async-start | bytes 4866048 | tf_op jit(solution)/shard_map/all_gather | solution.py:64
  152.8 211.8 %all-gather.17.cloned.1.call-start = ((), (), s32[]{:S(2)}) async-start(), calls=%async_computation.16 | async-start | bytes 1966080 | tf_op jit(solution)/shard_map/all_gather | solution.py:158
  155.6 77.6 %copy-start.97 = (f32[3072]{0:T(1024)S(1)}, f32[3072]{0:T(1024)}, u32[]{:S(2)}) copy-start(f32[3072]{0:T(1024)} %slice.116) | copy-start | bytes 36868
  246.9 56.4 %copy-start.5 = (bf16[128,2,3072]{2,0,1:T(8,128)(2,1)}, bf16[128,2,3072]{2,0,1:T(8,128)(2,1)S(1)}, u32[]{:S(2)}) copy-start(bf16[128,2,3072]{2,0,1:T(8,128)(2,1)S(1)} %fusion.52) | copy-start | bytes 4718596
  346.5 61.4 %all-gather.15.cloned.1.call-start = ((), (), s32[]{:S(2)}) async-start(), calls=%async_computation.14 | async-start | bytes 1966080 | tf_op jit(solution)/shard_map/all_gather | solution.py:158
  348.5 217.3 %reduce-scatter.13.cloned.1.call-start = ((), (), s32[]{:S(2)}) async-start(), calls=%async_computation.17 | async-start | bytes 1966080 | tf_op jit(solution)/shard_map/reduce_scatter | solution.py:185
  407.4 159.5 %reduce-scatter.11.cloned.1.call-start = ((), (), s32[]{:S(2)}) async-start(), calls=%async_computation.15 | async-start | bytes 1966080 | tf_op jit(solution)/shard_map/reduce_scatter | solution.py:185
  450.6 170.8 %reduce-scatter.17.cloned.1.call-start = ((), (), s32[]{:S(2)}) async-start(), calls=%async_computation.19 | async-start | bytes 9732096 | tf_op jit(solution)/shard_map/reduce_scatter | solution.py:78
  459.9 303.7 %reduce-scatter.15.cloned.1.call-start = ((), (), s32[]{:S(2)}) async-start(), calls=%async_computation.18 | async-start | bytes 9732096 | tf_op jit(solution)/shard_map/reduce_scatter | solution.py:77
  479.8 17.9 %all-to-all-start.1 = ((bf16[8,192,96]{2,1,0:T(8,128)(2,1)}), bf16[8,192,96]{2,1,0:T(8,128)(2,1)S(1)}, u32[]{:S(2)}, u32[]{:S(2)}) async-start(bf16[8,192,96]{2,1,0:T(8,128)(2,1)} %bitcast.207), calls=%async_computation.5 | async-start | bytes 786432 | tf_op jit(solution)/shard_map/all_to_all | solution.py:30
  489.8 67.5 %copy-start.109 = (f32[288]{0:T(512)S(1)}, f32[288]{0:T(512)}, u32[]{:S(2)}) copy-start(f32[288]{0:T(512)} %param.25) | copy-start | bytes 3460
  491.0 68.4 %copy-start.52 = (f32[192,96]{1,0:T(8,128)S(1)}, f32[192,96]{1,0:T(8,128)}, u32[]{:S(2)}) copy-start(f32[192,96]{1,0:T(8,128)} %param.22) | copy-start | bytes 221188
  491.1 68.4 %copy-start.60 = (f32[192,96]{1,0:T(8,128)S(1)}, f32[192,96]{1,0:T(8,128)}, u32[]{:S(2)}) copy-start(f32[192,96]{1,0:T(8,128)} %param.32) | copy-start | bytes 221188
  491.1 68.4 %copy-start.61 = (f32[192,96]{1,0:T(8,128)S(1)}, f32[192,96]{1,0:T(8,128)}, u32[]{:S(2)}) copy-start(f32[192,96]{1,0:T(8,128)} %param.27) | copy-start | bytes 221188
  492.4 69.0 %copy-start.47 = (f32[3,96,192]{1,2,0:T(8,128)S(1)}, f32[3,96,192]{1,2,0:T(8,128)}, u32[]{:S(2)}) copy-start(f32[3,96,192]{1,2,0:T(8,128)} %copy.153) | copy-start | bytes 663556
  492.4 69.0 %copy-start.48 = (f32[3,96,192]{1,2,0:T(8,128)S(1)}, f32[3,96,192]{1,2,0:T(8,128)}, u32[]{:S(2)}) copy-start(f32[3,96,192]{1,2,0:T(8,128)} %copy.152) | copy-start | bytes 663556
  492.4 69.0 %copy-start.49 = (f32[3,96,192]{1,2,0:T(8,128)S(1)}, f32[3,96,192]{1,2,0:T(8,128)}, u32[]{:S(2)}) copy-start(f32[3,96,192]{1,2,0:T(8,128)} %copy.154) | copy-start | bytes 663556
  497.6 62.6 %all-to-all-start = ((bf16[8,3,96,192]{2,3,1,0:T(8,128)(2,1)}), bf16[8,3,96,192]{2,3,1,0:T(8,128)(2,1)S(1)}, u32[]{:S(2)}, u32[]{:S(2)}) async-start(bf16[8,3,96,192]{2,3,1,0:T(8,128)(2,1)} %bitcast.206), calls=%async_computation.4 | async-start | bytes 2359296 | tf_op jit(solution)/shard_map/all_to_all | solution.py:30
  568.0 53.4 %copy-start.44 = (f32[96,768]{1,0:T(8,128)S(1)}, f32[96,768]{1,0:T(8,128)}, u32[]{:S(2)}) copy-start(f32[96,768]{1,0:T(8,128)} %param.24) | copy-start | bytes 884740
  568.0 53.4 %copy-start.54 = (f32[96,768]{1,0:T(8,128)S(1)}, f32[96,768]{1,0:T(8,128)}, u32[]{:S(2)}) copy-start(f32[96,768]{1,0:T(8,128)} %param.34) | copy-start | bytes 884740
  568.2 195.4 %copy-start.46 = (f32[768,96]{0,1:T(8,128)S(1)}, f32[768,96]{0,1:T(8,128)}, u32[]{:S(2)}) copy-start(f32[768,96]{0,1:T(8,128)} %param.23) | copy-start | bytes 884740
  568.2 195.4 %copy-start.56 = (f32[768,96]{0,1:T(8,128)S(1)}, f32[768,96]{0,1:T(8,128)}, u32[]{:S(2)}) copy-start(f32[768,96]{0,1:T(8,128)} %param.33) | copy-start | bytes 884740
  568.2 195.4 %copy-start.57 = (f32[768,96]{0,1:T(8,128)S(1)}, f32[768,96]{0,1:T(8,128)}, u32[]{:S(2)}) copy-start(f32[768,96]{0,1:T(8,128)} %param.28) | copy-start | bytes 884740
  (119 other events, 850.3 us)
Sparse Core Ops, SparseCore 0:
  11.2 22.5 all-gather.6
  35.3 20.1 all-gather.12
  139.4 37.0 reduce-scatter.6
  179.0 38.1 reduce-scatter.8
  346.6 17.9 all-gather.16
  366.0 19.6 all-gather.14
  407.5 28.3 reduce-scatter.12
  450.7 28.3 reduce-scatter.10
  485.6 135.8 reduce-scatter.16
  628.8 134.7 reduce-scatter.14
Sparse Core Ops, SparseCore 1:
  155.2 77.8 all-gather.8
  236.5 62.5 all-gather.10
where the time goes:
time: 775 us; the launch traced here: 773 us
  waiting for transfers between devices  339 us (44%)
  blocking collectives  154 us (20%)
  matrix products  146 us (19%)
  other arithmetic  53 us (7%)
  local copies, waits for them, and re-layouts  52.2 us (7%)
  between operations  17.7 us (2%)
  starting transfers between devices  10.8 us (1%)
    reduce_scatter x1, waiting for transfers between devices, reduce_grads(): lax.psum_scatter(grad_up, ('dp', 'head'), scatter_dimension=1, tiled=True)  140 us
    unnamed x2, blocking collectives  85.2 us
    reduce_scatter x2, waiting for transfers between devices, micro_pass(): lax.psum_scatter(jnp.einsum('lbk,kd->lbd', piece, attn_out, preferred_ele...  61.7 us
    all_gather x1, waiting for transfers between devices, fetch_weights(): lax.all_gather(w_down.astype(jnp.bfloat16), ('dp', 'head'), axis=0, tiled...  52.2 us
    reduce_scatter x1, waiting for transfers between devices, reduce_grads(): lax.psum_scatter(grad_down, ('dp', 'head'), scatter_dimension=0, tiled=True)  51.1 us
    all_gather x1, blocking collectives, fetch_weights(): lax.all_gather(w_qkv.astype(jnp.bfloat16), 'dp', axis=1, tiled=True)  38 us
    unnamed x304, local copies, waits for them, and re-layouts  37.3 us
    all_gather x1, blocking collectives, fetch_weights(): lax.all_gather(w_out.astype(jnp.bfloat16), 'dp', axis=1, tiled=True)  31.1 us
  transfers between devices with their start and end apart: 14, of which 8 were waited for; matrix products, arithmetic and copies ran while one was open for 25% of the time, Pallas kernels for 0%

commit v1 on v0

v1 whole, which is shorter than its diff:
```python
import functools
import math

import jax
import jax.numpy as jnp
from jax import lax
from jax.experimental import pallas as pl
from jax.experimental.pallas import tpu as pltpu
from jax.sharding import Mesh
from jax.sharding import PartitionSpec as P

D = 768
HD = 64
FF = 3072
LEN = 512

EPSILON = 1e-05
MOMENTUM = 0.9
AVERAGE = 0.9
DECAY = 0.01
RATE_BASE = 0.05

BF = jnp.bfloat16
F32 = jnp.float32
NT = (((1,), (1,)), ((), ()))
NN = (((1,), (0,)), ((), ()))
DIM = {"c": 0, "x": 1, "y": 2, "z": 3}


def send(values, axis, shift):
    size = lax.axis_size(axis)
    return lax.ppermute(values, axis, [(i, (i + shift) % size) for i in range(size)])


def flip_order(axis):
    size = lax.axis_size(axis)
    return (lax.axis_index(axis) - jnp.arange(size)) % size


def gather_axis(values, axis):
    dim = DIM[axis]
    size = lax.axis_size(axis)
    if size > 4:
        whole = lax.all_gather(values, axis, axis=dim, tiled=True)
        return jnp.take(whole, flip_order(axis), axis=dim)
    return jnp.concatenate([values] + [send(values, axis, k) for k in range(1, size)], dim)


def gather(shard, order):
    values = shard[None, None, None, None]
    for axis in order:
        values = gather_axis(values, axis)
    return values


def scatter_axis(values, axis, last):
    dim = DIM[axis]
    size = lax.axis_size(axis)
    if size > 4:
        whole = jnp.take(values, flip_order(axis), axis=dim)
        parts = lax.all_to_all(whole, axis, dim, dim, tiled=True)
        total = jnp.sum(parts.astype(F32), dim, keepdims=True)
    else:
        part = lambda k: lax.slice_in_dim(values, k, k + 1, axis=dim)
        total = part(0).astype(F32)
        for k in range(1, size):
            total = total + send(part(k), axis, -k).astype(F32)
    return total if last else total.astype(BF)


def scatter(values, order):
    for axis in order:
        values = scatter_axis(values, axis, axis == order[-1])
    return values[0, 0, 0, 0]


def to_documents(values):
    y, c = lax.axis_index("y"), lax.axis_index("c")
    docs = values.transpose(1, 0, 2).reshape(2, 2, values.shape[0], values.shape[2])
    mine = lax.dynamic_index_in_dim(docs, y, 0, keepdims=False)
    theirs = lax.dynamic_index_in_dim(docs, 1 - y, 0, keepdims=False)
    pair = jnp.stack([mine, send(theirs, "y", 1)], 1)
    own = lax.dynamic_index_in_dim(pair, c, 0, keepdims=False)
    other = lax.dynamic_index_in_dim(pair, 1 - c, 0, keepdims=False)
    return jnp.stack([own, send(other, "c", 1)], 0)


def from_documents(values):
    y, c = lax.axis_index("y"), lax.axis_index("c")
    got = send(values[1], "c", 1)
    pair = jnp.stack([jnp.where(c == 0, values[0], got), jnp.where(c == 0, got, values[0])], 0)
    got = send(pair[:, 1], "y", 1)
    own = pair[:, 0]
    docs = jnp.stack([jnp.where(y == 0, own, got), jnp.where(y == 0, got, own)], 0)
    return docs.reshape(4, docs.shape[2], docs.shape[3]).transpose(1, 0, 2)


def dot(a, b, dims):
    return lax.dot_general(a, b, dims, preferred_element_type=F32)


def place_weights(place_ref, source, target, rows):
    across, deep = source.shape[1], source.shape[3]
    for i in range(across):
        for k in range(deep):
            start = place_ref[i * deep + k] * rows
            if rows % 32 == 0:
                start = pl.multiple_of(start, 32)
            target[pl.ds(start, rows), :] = source[0, i, 0, k, :rows]


def forward_kernel(
    rows,
    place_ref,
    x_ref,
    qk_ref,
    vo_ref,
    bias_ref,
    mask_ref,
    qkv_ref,
    lse_ref,
    context_ref,
    mix_ref,
    w_qk,
    w_vo,
):
    step = pl.program_id(0)
    place_weights(place_ref, qk_ref, w_qk, rows)
    place_weights(place_ref, vo_ref, w_vo, rows)
    x = x_ref[...]
    width = w_qk.shape[1] // 2
    bias = bias_ref[0]
    qk = dot(x, w_qk[...], NN)
    v = (dot(x, w_vo[:, :width], NN) + bias[1:2, :width]).astype(BF)
    q = ((qk[:, :width] + bias[0:1, :width]).astype(BF).astype(F32) * HD ** (-0.5)).astype(BF)
    k = qk[:, width:].astype(BF)
    qkv_ref[0, :, :width] = q
    qkv_ref[0, :, width : 2 * width] = k
    qkv_ref[0, :, 2 * width :] = v
    mask = mask_ref[...]
    length = x.shape[0]
    contexts, logs = [], []
    for head in range(width // HD):
        cols = slice(head * HD, (head + 1) * HD)
        s = dot(q[:, cols], k[:, cols], NT) + mask
        peak = jnp.max(s, -1, keepdims=True)
        total = jnp.sum(jnp.exp(s - peak), -1, keepdims=True)
        log_total = peak + jnp.log(total)
        p = jnp.exp(s - log_total).astype(BF)
        contexts.append(dot(p, v[:, cols], NN).astype(BF))
        logs.append(log_total)
    context = jnp.concatenate(contexts, 1)
    context_ref[0] = context
    lanes = lax.broadcasted_iota(jnp.int32, (length, 128), 1)
    packed = jnp.zeros((length, 128), F32)
    for head, log_total in enumerate(logs):
        packed = jnp.where(lanes == head, log_total, packed)
    lse_ref[0] = packed.T[:8]
    mix = dot(context, w_vo[:, width:], NT)

    @pl.when(step == 0)
    def _():
        mix_ref[...] = mix

    @pl.when(step > 0)
    def _():
        mix_ref[...] += mix


def backward_kernel(
    rows,
    place_ref,
    x_ref,
    gr_ref,
    qk_ref,
    vo_ref,
    qkv_ref,
    lse_ref,
    context_ref,
    mask_ref,
    gqk_ref,
    gvo_ref,
    bias_ref,
    gin_ref,
    w_qk,
    w_vo,
    x_t,
    gr_t,
    g_qkv,
):
    step = pl.program_id(0)
    place_weights(place_ref, qk_ref, w_qk, rows)
    place_weights(place_ref, vo_ref, w_vo, rows)

    @pl.when(step == 0)
    def _():
        x_t[...] = x_ref[...].T
        gr_t[...] = gr_ref[...].T

    width = w_qk.shape[1] // 2
    gr = gr_ref[...]
    gc = dot(gr, w_vo[:, width:], NN).astype(BF)
    mask = mask_ref[:, :1]
    sums = []
    for head in range(width // HD):
        q = qkv_ref[0, :, head * HD : (head + 1) * HD]
        k = qkv_ref[0, :, width + head * HD : width + (head + 1) * HD]
        v = qkv_ref[0, :, 2 * width + head * HD : 2 * width + (head + 1) * HD]
        g = gc[:, head * HD : (head + 1) * HD]
        p = jnp.exp(dot(k, q, NT) + mask - lse_ref[0, head : head + 1])
        dp = dot(v, g, NT)
        gv = dot(p.astype(BF), g, NN)
        delta = jnp.sum(p * dp, 0, keepdims=True)
        gs = (p * (dp - delta)).astype(BF)
        gk = dot(gs, q, NN)
        gq = dot(gs.T, (k.astype(F32) * HD ** (-0.5)).astype(BF), NN)
        g_qkv[:, head * HD : (head + 1) * HD] = gq.astype(BF)
        g_qkv[:, width + head * HD : width + (head + 1) * HD] = gk.astype(BF)
        g_qkv[:, 2 * width + head * HD : 2 * width + (head + 1) * HD] = gv.astype(BF)
        sums.append((jnp.sum(gq, 0, keepdims=True), jnp.sum(gv, 0, keepdims=True)))
    bias_ref[0, 0:1, :] = jnp.concatenate([s[0] for s in sums], 1)
    bias_ref[0, 1:2, :] = jnp.concatenate([s[1] for s in sums], 1)
    g_qk = g_qkv[:, : 2 * width]
    g_v = g_qkv[:, 2 * width :]
    gin = dot(g_qk, w_qk[...], NT) + dot(g_v, w_vo[:, :width], NT)

    @pl.when(step == 0)
    def _():
        gin_ref[...] = gin

    @pl.when(step > 0)
    def _():
        gin_ref[...] += gin

    w_qk[...] = dot(x_t[...], g_qk, NN).astype(BF)
    w_vo[:, :width] = dot(x_t[...], g_v, NN).astype(BF)
    w_vo[:, width:] = dot(gr_t[...], context_ref[0], NN).astype(BF)
    across, deep = gqk_ref.shape[1], gqk_ref.shape[3]
    for i in range(across):
        for j in range(deep):
            start = place_ref[i * deep + j] * rows
            if rows % 32 == 0:
                start = pl.multiple_of(start, 32)
            gqk_ref[0, i, 0, j, :rows] = w_qk[pl.ds(start, rows), :]
            gvo_ref[0, i, 0, j] = w_vo[pl.ds(start, rows), :]


def whole(shape):
    return pl.BlockSpec(shape, lambda g: (0,) * len(shape))


def per_group(array):
    rest = array[1:]
    return pl.BlockSpec((1, *rest), lambda g: (g, *(0 for _ in rest)))


def per_corner(shape, rows):
    return pl.BlockSpec(
        (1, shape[1], 1, shape[3], rows, shape[5]), lambda g: (g // 2, 0, g % 2, 0, 0, 0)
    )


def attention_forward(place, x, w_qk, w_vo, biases, mask_row, rows):
    length = x.shape[0]
    pair = w_qk.shape[5]
    width = pair // 2
    outs = [
        jax.ShapeDtypeStruct((4, length, 3 * width), BF),
        jax.ShapeDtypeStruct((4, 8, length), F32),
        jax.ShapeDtypeStruct((4, length, width), BF),
        jax.ShapeDtypeStruct((length, D), F32),
    ]
    return pl.pallas_call(
        functools.partial(forward_kernel, rows),
        grid=(4,),
        in_specs=[
            pl.BlockSpec(memory_space=pltpu.SMEM),
            whole(x.shape),
            per_corner(w_qk.shape, rows),
            per_corner(w_vo.shape, rows),
            per_group(biases.shape),
            whole(mask_row.shape),
        ],
        out_specs=[per_group(o.shape) for o in outs[:3]] + [whole(outs[3].shape)],
        out_shape=outs,
        scratch_shapes=[pltpu.VMEM((D, pair), BF), pltpu.VMEM((D, pair), BF)],
        compiler_params=pltpu.CompilerParams(vmem_limit_bytes=32 << 20),
        cost_estimate=pl.CostEstimate(
            flops=9_000_000_000, bytes_accessed=12_000_000, transcendentals=6_300_000
        ),
        name="attention_forward",
    )(place, x, w_qk, w_vo, biases, mask_row)


def attention_backward(place, x, gr, w_qk, w_vo, qkv, lse, context, mask_col, rows, extra):
    length = x.shape[0]
    pair = w_qk.shape[5]
    width = pair // 2
    lead = w_qk.shape[:4]
    outs = [
        jax.ShapeDtypeStruct((*lead, rows + extra, pair), BF),
        jax.ShapeDtypeStruct((*lead, rows, pair), BF),
        jax.ShapeDtypeStruct((4, 8, width), F32),
        jax.ShapeDtypeStruct((length, D), F32),
    ]
    return pl.pallas_call(
        functools.partial(backward_kernel, rows),
        grid=(4,),
        in_specs=[
            pl.BlockSpec(memory_space=pltpu.SMEM),
            whole(x.shape),
            whole(gr.shape),
            per_corner(w_qk.shape, rows),
            per_corner(w_vo.shape, rows),
            per_group(qkv.shape),
            per_group(lse.shape),
            per_group(context.shape),
            whole(mask_col.shape),
        ],
        out_specs=[
            per_corner(outs[0].shape, rows + extra),
            per_corner(outs[1].shape, rows),
            per_group(outs[2].shape),
            whole(outs[3].shape),
        ],
        out_shape=outs,
        scratch_shapes=[
            pltpu.VMEM((D, pair), BF),
            pltpu.VMEM((D, pair), BF),
            pltpu.VMEM((D, length), BF),
            pltpu.VMEM((D, length), BF),
            pltpu.VMEM((length, 3 * width), BF),
        ],
        compiler_params=pltpu.CompilerParams(vmem_limit_bytes=40 << 20),
        cost_estimate=pl.CostEstimate(
            flops=18_000_000_000, bytes_accessed=16_000_000, transcendentals=3_200_000
        ),
        name="attention_backward",
    )(place, x, gr, w_qk, w_vo, qkv, lse, context, mask_col)


def norm_forward(values, gain, shift):
    center = values - jnp.mean(values, -1, keepdims=True)
    inverse = lax.rsqrt(jnp.mean(center * center, -1, keepdims=True) + EPSILON)
    normed = center * inverse
    return (normed * gain + shift, normed, inverse)


def norm_backward(d_result, normed, inverse, gain):
    d_normed = d_result * gain
    return inverse * (
        d_normed
        - jnp.mean(d_normed, -1, keepdims=True)
        - normed * jnp.mean(d_normed * normed, -1, keepdims=True)
    )


def gelu_slope(values):
    return (
        0.5 * (1.0 + lax.erf(values * 0.7071067811865476))
        + values * jnp.exp(-0.5 * values * values) * 0.3989422804014327
    )


def advance(weight, grad, moment, average, decay, rate):
    step_grad = grad + decay * weight
    moment_new = MOMENTUM * moment + step_grad
    weight_new = weight - rate * (step_grad + MOMENTUM * moment_new)
    average_new = AVERAGE * average + (1.0 - AVERAGE) * weight_new
    return (weight_new, moment_new, average_new)


def body(
    layer_input,
    lengths,
    cotangent,
    w_qkv,
    w_out,
    w_up,
    w_down,
    vectors,
    mom_qkv,
    mom_out,
    mom_up,
    mom_down,
    mom_vec,
    avg_qkv,
    avg_out,
    avg_up,
    avg_down,
    avg_vec,
):
    z, x, y, c = (lax.axis_index(a) for a in ("z", "x", "y", "c"))
    deep = lax.axis_size("z")
    blocks = deep * 8
    rows, head_cols = w_qkv.shape[1], w_qkv.shape[2]
    pair = 2 * head_cols
    vec_len = vectors.shape[0]
    ff_rows = w_up.shape[1]
    local = layer_input.shape[0]
    length = 4 * local

    kc, kx, ky, kz = jnp.meshgrid(
        jnp.arange(2), jnp.arange(2), jnp.arange(2), jnp.arange(deep), indexing="ij"
    )
    owner = ((((z - kz) % deep) * 2 + (x ^ kx)) * 4 + (y ^ ky) * 2 + (c ^ kc)).reshape(blocks)
    tz, tx, ty, tc = jnp.meshgrid(
        jnp.arange(deep), jnp.arange(2), jnp.arange(2), jnp.arange(2), indexing="ij"
    )
    seat = ((((c ^ tc) * 2 + (x ^ tx)) * 2 + (y ^ ty)) * deep + (z - tz) % deep).reshape(blocks)
    group_c, group_y = jnp.meshgrid(jnp.arange(2), jnp.arange(2), indexing="ij")
    group_head = ((y ^ group_y) * 2 + (c ^ group_c)).reshape(4)
    head_group = ((c ^ group_y) * 2 + (y ^ group_c)).reshape(4)

    vec_row = jnp.pad(vectors.astype(BF), (0, pair - vec_len))[None]
    pack_qk = jnp.concatenate(
        [jnp.concatenate([w_qkv[0], w_qkv[1]], 1).astype(BF), vec_row], 0
    )
    pack_vo = jnp.concatenate([w_qkv[2], w_out.T], 1).astype(BF)
    doc_x = to_documents(layer_input).reshape(length, D)
    full_qk = gather(pack_qk, ("z", "y", "x", "c"))
    full_vo = gather(pack_vo, ("z", "x", "y", "c"))
    full_up = gather(w_up.T.astype(BF), ("z", "y", "x", "c")).reshape(FF, D)
    full_down = gather(w_down.astype(BF), ("z", "x", "y", "c")).reshape(FF, D)
    doc_cot = to_documents(cotangent).reshape(length, D)

    vec_all = full_qk[..., rows, :vec_len].reshape(blocks, vec_len).astype(F32)
    vec_rows = jnp.take(vec_all, seat, axis=0).reshape(12, D)
    bias_up = jnp.take(vec_rows[5:9].reshape(blocks, ff_rows), owner, axis=0).reshape(FF)
    bias_q = jnp.take(vec_rows[0].reshape(4, head_cols), group_head, axis=0)
    bias_v = jnp.take(vec_rows[1].reshape(4, head_cols), group_head, axis=0)
    biases = jnp.pad(jnp.stack([bias_q, bias_v], 1), ((0, 0), (0, 6), (0, 0)))

    row = jnp.arange(length)
    part = row // local
    position = ((y ^ (part % 2)) * 2 + (c ^ (part // 2))) * local + row % local
    doc_len = lax.dynamic_index_in_dim(lengths, y * 2 + c, 0, keepdims=False)
    alive = position < doc_len
    mask = jnp.where(alive, 0.0, -1e30).astype(F32)

    in_kernel = rows % 32 == 0 and deep <= 4
    if in_kernel:
        place = (((z - jnp.arange(deep)[None, :]) % deep) * 2 + (x ^ jnp.arange(2)[:, None])).reshape(
            2 * deep
        )
        attn_qk, attn_vo, kernel_rows = full_qk, full_vo, rows
    else:
        xs = x ^ jnp.arange(2)
        zs = flip_order("z")

        def true_order(values):
            values = jnp.take(jnp.take(values[..., :rows, :], xs, axis=1), zs, axis=3)
            return values.transpose(0, 2, 3, 1, 4, 5).reshape(2, 1, 2, 1, D, pair)

        place = jnp.zeros((1,), jnp.int32)
        attn_qk, attn_vo, kernel_rows = true_order(full_qk), true_order(full_vo), D
    place = place.astype(jnp.int32)

    qkv, lse, context, mix = attention_forward(
        place, doc_x, attn_qk, attn_vo, biases, mask[None, :], kernel_rows
    )
    first_res = doc_x.astype(F32) + mix + vec_rows[2]
    hidden_one, normed_one, inverse_one = norm_forward(first_res, vec_rows[3], vec_rows[4])
    hidden_b = hidden_one.astype(BF)
    up_pre = lax.dot_general(hidden_b, full_up, NT, preferred_element_type=F32) + bias_up
    act_b = jax.nn.gelu(up_pre, approximate=False).astype(BF)
    second_res = hidden_one + (
        lax.dot_general(act_b, full_down, NN, preferred_element_type=F32) + vec_rows[9]
    )
    result, normed_two, inverse_two = norm_forward(second_res, vec_rows[10], vec_rows[11])
    layer_output = from_documents(result.astype(BF).reshape(2, 2, local, D))

    d_result = jnp.where(alive[:, None], doc_cot.astype(F32), 0.0)
    d_gain_two = jnp.sum(d_result * normed_two, 0)
    d_shift_two = jnp.sum(d_result, 0)
    d_second = norm_backward(d_result, normed_two, inverse_two, vec_rows[10])
    d_bias_down = jnp.sum(d_second, 0)
    d_second_b = d_second.astype(BF)
    lead = (2, 2, 2, deep, ff_rows, D)
    grad_down = lax.dot_general(
        act_b, d_second_b, (((0,), (0,)), ((), ())), preferred_element_type=F32
    )
    grad_down = scatter(grad_down.astype(BF).reshape(lead), ("c", "y", "x", "z"))
    d_act = lax.dot_general(d_second_b, full_down, NT, preferred_element_type=F32)
    d_up = d_act * gelu_slope(up_pre)
    d_bias_up = jnp.sum(d_up, 0)
    d_up_b = d_up.astype(BF)
    grad_up = lax.dot_general(
        d_up_b, hidden_b, (((0,), (0,)), ((), ())), preferred_element_type=F32
    )
    grad_up = scatter(grad_up.astype(BF).reshape(lead), ("c", "x", "y", "z")).T
    d_hidden = d_second + lax.dot_general(d_up_b, full_up, NN, preferred_element_type=F32)
    d_gain_one = jnp.sum(d_hidden * normed_one, 0)
    d_shift_one = jnp.sum(d_hidden, 0)
    d_first = norm_backward(d_hidden, normed_one, inverse_one, vec_rows[3])
    d_bias_out = jnp.sum(d_first, 0)
    d_first_b = d_first.astype(BF)

    mask_col = jnp.broadcast_to(mask[:, None], (length, 128))
    grad_qk, grad_vo, d_bias, d_attn = attention_backward(
        place, doc_x, d_first_b, attn_qk, attn_vo, qkv, lse, context, mask_col, kernel_rows, 8
    )
    grad_input = from_documents((d_first + d_attn).astype(BF).reshape(2, 2, local, D)).astype(F32)

    if not in_kernel:

        def relative_order(values):
            values = values[..., :D, :].reshape(2, 2, deep, 2, rows, pair)
            values = values.transpose(0, 3, 1, 2, 4, 5)
            return jnp.take(jnp.take(values, xs, axis=1), zs, axis=3)

        grad_qk, grad_vo = relative_order(grad_qk), relative_order(grad_vo)
        grad_qk = jnp.pad(grad_qk, ((0, 0),) * 4 + ((0, 8), (0, 0)))

    d_bias_q = jnp.take(d_bias[:, 0], head_group, axis=0).reshape(D)
    d_bias_v = jnp.take(d_bias[:, 1], head_group, axis=0).reshape(D)
    d_bias_up = jnp.take(d_bias_up.reshape(blocks, ff_rows), seat, axis=0).reshape(FF)
    grad_vec = jnp.concatenate(
        [
            d_bias_q,
            d_bias_v,
            d_bias_out,
            d_gain_one,
            d_shift_one,
            d_bias_up,
            d_bias_down,
            d_gain_two,
            d_shift_two,
        ]
    )
    vec_part = jnp.take(grad_vec.reshape(blocks, vec_len), owner, axis=0).astype(BF)
    vec_part = jnp.pad(vec_part, ((0, 0), (0, pair - vec_len))).reshape(2, 2, 2, deep, 1, pair)
    vec_part = jnp.pad(vec_part, ((0, 0),) * 4 + ((0, 7), (0, 0)))
    grad_qk = lax.dynamic_update_slice(grad_qk, vec_part, (0, 0, 0, 0, rows, 0))
    sum_vo = scatter(grad_vo, ("c", "y", "x", "z"))
    sum_qk = scatter(grad_qk, ("c", "x", "y", "z"))
    grad_qkv = jnp.stack(
        [sum_qk[:rows, :head_cols], sum_qk[:rows, head_cols:], sum_vo[:, :head_cols]]
    )
    grad_out = sum_vo[:, head_cols:].T
    grad_vec = sum_qk[rows, :vec_len]

    slots = local * 4 * layer_input.shape[1] * deep * 2
    rate = RATE_BASE / math.sqrt(slots)
    rate_out = rate * math.sqrt(LEN / 8.0)
    new_qkv, new_mom_qkv, new_avg_qkv = advance(w_qkv, grad_qkv, mom_qkv, avg_qkv, DECAY, rate)
    new_out, new_mom_out, new_avg_out = advance(w_out, grad_out, mom_out, avg_out, DECAY, rate_out)
    new_up, new_mom_up, new_avg_up = advance(w_up, grad_up, mom_up, avg_up, DECAY, rate)
    new_down, new_mom_down, new_avg_down = advance(
        w_down, grad_down, mom_down, avg_down, DECAY, rate
    )
    new_vec, new_mom_vec, new_avg_vec = advance(vectors, grad_vec, mom_vec, avg_vec, 0.0, rate)
    return (
        layer_output,
        grad_input,
        grad_qkv,
        grad_out,
        grad_up,
        grad_down,
        grad_vec,
        new_qkv,
        new_out,
        new_up,
        new_down,
        new_vec,
        new_mom_qkv,
        new_mom_out,
        new_mom_up,
        new_mom_down,
        new_mom_vec,
        new_avg_qkv,
        new_avg_out,
        new_avg_up,
        new_avg_down,
        new_avg_vec,
    )


def solution(mesh):
    dp, head = mesh.shape["dp"], mesh.shape["head"]
    fine = Mesh(mesh.devices.reshape(dp // 2, 2, head // 2, 2), ("z", "x", "y", "c"))
    dps, heads, every = ("z", "x"), ("y", "c"), ("z", "x", "y", "c")
    acts = P(heads, dps, None)
    params = (P(None, dps, heads), P(heads, dps), P(None, every), P(every, None), P(every))
    return jax.shard_map(
        body,
        mesh=fine,
        in_specs=(acts, P(dps), acts) + params * 3,
        out_specs=(acts, acts) + params * 4,
        check_vma=False,
    )
```

time: 775 us -> 369 us (0.48)
  waiting for transfers between devices: 339 us -> 116 us
  blocking collectives: 154 us -> 0 us
  matrix products: 146 us -> 35.4 us
  starting transfers between devices: 10.8 us -> 64 us
  Pallas kernels: 0 us -> 35 us
  between operations: 17.7 us -> 2.91 us
    reduce_scatter x6 -> x0, waiting for transfers between devices: 253 us -> none  [the longest x1 140 us: reduce_grads(): lax.psum_scatter(grad_up, ('dp', 'head'), scatter_dimension=1, tiled=True)]
    ppermute x0 -> x56, waiting for transfers between devices: none -> 116 us  [send(): lax.ppermute(values, axis, [(i, (i + shift) % size) for i in range(size)])]
    dot_general x36 -> x6, matrix products: 146 us -> 35.4 us  [the longest x1 15.7 us: body(): lax.dot_general(hidden_b, full_up, NT, preferred_element_type=F32) + bias_up]
    unnamed x2 -> x0, blocking collectives: 85.2 us -> none
    all_gather x6 -> x0, waiting for transfers between devices: 81.5 us -> none  [the longest x1 52.2 us: fetch_weights(): lax.all_gather(w_down.astype(jnp.bfloat16), ('dp', 'head'), axis=0, tiled...]
    all_gather x2 -> x0, blocking collectives: 69.1 us -> none  [the longest x1 38 us: fetch_weights(): lax.all_gather(w_qkv.astype(jnp.bfloat16), 'dp', axis=1, tiled=True)]
    ppermute x0 -> x56, starting transfers between devices: none -> 64 us  [send(): lax.ppermute(values, axis, [(i, (i + shift) % size) for i in range(size)])]
    pallas_call x0 -> x2, Pallas kernels: none -> 35 us  [the longest x1 22.7 us: attention_backward(): pl.pallas_call(functools.partial(backward_kernel, rows), grid=(4,), in_sp...]
  transfers between devices with their start and end apart: 14 -> 56, of which waited for: 8 -> 21; matrix products, arithmetic and copies ran while one was open for 25% -> 30% of each run, Pallas kernels for 0% -> 10%
where the time goes in v1:
time: 369 us; the launch traced here: 363 us
  waiting for transfers between devices  116 us (31%)
  starting transfers between devices  64 us (17%)
  other arithmetic  58.1 us (16%)
  local copies, waits for them, and re-layouts  51.7 us (14%)
  matrix products  35.4 us (10%)
  Pallas kernels  35 us (9%)
    ppermute x56, waiting for transfers between devices, send(): lax.ppermute(values, axis, [(i, (i + shift) % size) for i in range(size)])  116 us
    ppermute x56, starting transfers between devices, send(): lax.ppermute(values, axis, [(i, (i + shift) % size) for i in range(size)])  64 us
    pallas_call x1, Pallas kernels, attention_backward(): pl.pallas_call(functools.partial(backward_kernel, rows), grid=(4,), in_sp...  22.7 us
    concatenate x16, other arithmetic, gather_axis(): jnp.concatenate([values] + [send(values, axis, k) for k in range(1, size)...  21.1 us
    dot_general x1, matrix products, body(): lax.dot_general(hidden_b, full_up, NT, preferred_element_type=F32) + bias_up  15.7 us
    unnamed x199, local copies, waits for them, and re-layouts  13.8 us
    pallas_call x1, Pallas kernels, attention_forward(): pl.pallas_call(functools.partial(forward_kernel, rows), grid=(4,), in_spe...  12.2 us
    slice x16, local copies, waits for them, and re-layouts, scatter_axis(): part = lambda k: lax.slice_in_dim(values, k, k + 1, axis=dim)  8.08 us
  transfers between devices with their start and end apart: 56, of which 21 were waited for; matrix products, arithmetic and copies ran while one was open for 30% of the time, Pallas kernels for 10%

profile of v1, /device:TPU:0, one launch (start us, length us, event | category | flops | bytes accessed | tf_op | source)
XLA Modules:
  0.0 363.3 jit_solution(8565173979591351163)
XLA Ops:
  1.7 5.1 %collective-permute-start.16 = (bf16[1,1,1,1,96,768]{5,4,3,2,1,0:T(8,128)(2,1)S(1)}, bf16[1,1,1,1,96,768]{5,4,3,2,1,0:T(8,128)(2,1)S(1)}, u32[]{:S(2)}, u32[]{:S(2)}) collective-permute-start(bf16[1,1,1,1,96,768]{5,4,3,2,1,0:T(8,128)(2,1)S(1)} %convert_bitcast_fusion.1), channel_id=1, source_target_pairs={{0,24},{8,0},{16,8},{24,16},{1,25},{9,1},{17,9},{25,17},{2,26},{10... | collective-permute-start | bytes 442376 | tf_op jit(solution)/shard_map/ppermute | solution.py:32
  10.6 2.8 collective-permute-start.10
  24.7 3.8 %collective-permute-start.22 = (bf16[1,1,1,1,96,768]{5,4,3,2,1,0:T(8,128)(2,1)S(1)}, bf16[1,1,1,1,96,768]{5,4,3,2,1,0:T(8,128)(2,1)S(1)}, u32[]{:S(2)}, u32[]{:S(2)}) collective-permute-start(bf16[1,1,1,1,96,768]{5,4,3,2,1,0:T(8,128)(2,1)S(1)} %convert_bitcast_fusion), channel_id=1, source_target_pairs={{0,24},{8,0},{16,8},{24,16},{1,25},{9,1},{17,9},{25,17},{2,26},{10... | collective-permute-start | bytes 442376 | tf_op jit(solution)/shard_map/ppermute | solution.py:32
  37.7 5.7 %collective-permute-done.21 = bf16[1,1,1,1,96,768]{5,4,3,2,1,0:T(8,128)(2,1)S(1)} collective-permute-done((bf16[1,1,1,1,96,768]{5,4,3,2,1,0:T(8,128)(2,1)S(1)}, bf16[1,1,1,1,96,768]{5,4,3,2,1,0:T(8,128)(2,1)S(1)}, u32[]{:S(2)}, u32[]{:S(2)}) %collective-permute-start.21) | collective-permute-done | bytes 147488 | tf_op jit(solution)/shard_map/ppermute | solution.py:32
  72.4 3.9 %collective-permute-done.12 = bf16[1,2,1,4,96,384]{5,4,3,2,1,0:T(8,128)(2,1)} collective-permute-done((bf16[1,2,1,4,96,384]{5,4,3,2,1,0:T(8,128)(2,1)}, bf16[1,2,1,4,96,384]{5,4,3,2,1,0:T(8,128)(2,1)}, u32[]{:S(2)}, u32[]{:S(2)}) %collective-permute-start.12) | collective-permute-done | bytes 589856 | tf_op jit(solution)/shard_map/ppermute | solution.py:32
  77.7 6.9 %collective-permute-done.28 = bf16[2,128,768]{2,1,0:T(8,128)(2,1)S(1)} collective-permute-done((bf16[2,128,768]{2,1,0:T(8,128)(2,1)}, bf16[2,128,768]{2,1,0:T(8,128)(2,1)S(1)}, u32[]{:S(2)}, u32[]{:S(2)}) %collective-permute-start.28) | collective-permute-done | bytes 393248 | tf_op jit(solution)/shard_map/ppermute | solution.py:32
  86.8 11.8 %collective-permute-done.6 = bf16[1,1,2,4,97,384]{5,3,4,2,1,0:T(4,128)(2,1)S(1)} collective-permute-done((bf16[1,1,2,4,97,384]{5,3,4,2,1,0:T(4,128)(2,1)S(1)}, bf16[1,1,2,4,97,384]{5,3,4,2,1,0:T(4,128)(2,1)S(1)}, u32[]{:S(2)}, u32[]{:S(2)}) %collective-permute-start.6) | collective-permute-done | bytes 596000 | tf_op jit(solution)/shard_map/ppermute | solution.py:32
  100.2 2.8 pad_maximum_fusion.4
  103.2 3.5 collective-permute-done.24
  124.9 12.2 %attention_forward.1 = (bf16[4,512,576]{2,1,0:T(8,128)(2,1)S(1)}, f32[4,8,512]{2,1,0:T(8,128)S(1)}, bf16[4,512,192]{2,1,0:T(8,128)(2,1)S(1)}, f32[512,768]{1,0:T(8,128)S(1)}) custom-call(s32[8]{0:T(128)S(1)} %add.489.place_ref, bf16[512,768]{1,0:T(8,128)(2,1)S(1)} %bitcast.158, bf16[2,2,2,4,97,384]{5,4,3,2,1,0:T(8,128)(2,1)S(1)} %pad_maximum_fusion.2.qk_ref, ...), custom_call_target="tpu_custom_call" | custom-call | flops 8999999488 | bytes 12000000 | tf_op jit(solution)/shard_map/attention_forward/pallas_call | solution.py:273
  140.3 3.3 pad_maximum_fusion
  143.7 15.7 %fusion.2 = (bf16[512,3072]{1,0:T(8,128)(2,1)S(1)}, f32[512,3072]{1,0:T(8,128)S(1)}) fusion(f32[3072]{0:T(1024)S(1)} %add.515, bf16[3072,768]{1,0:T(8,128)(2,1)S(1)} %bitcast.164, f32[512,768]{1,0:T(8,128)S(1)} %get-tuple-element.150, f32[768]{0:T(1024)S(1)} %copy-done.83, f32[768]{0:T(1024)S(1)} %get-tuple-element.119, f32[512]{0:T(512)S(1)} %add_rsqrt_fusion.1, ...), kind=kOutput, calls=%fused_computation.12 | convolution fusion | flops 2521694208 | bytes 15751168 | tf_op jit(solution)/shard_map/dot_general | solution.py:465
  162.1 2.8 fusion.90
  168.7 4.6 %fusion.91 = (f32[3072]{0:T(1024)S(1)}, bf16[512,3072]{1,0:T(8,128)(2,1)S(1)}) fusion(f32[512,3072]{1,0:T(8,128)S(1)} %get-tuple-element.204, f32[3072]{0:T(1024)S(1)} %copy-done.73, bf16[3072,768]{1,0:T(8,128)(2,1)S(1)} %bitcast.167, f32[512,768]{1,0:T(8,128)S(1)} %get-tuple-element.142), kind=kOutput, calls=%fused_computation.327 | convolution fusion | flops 2435183616 | bytes 15753216 | tf_op jit(solution)/shard_map/dot_general | solution.py:484
  173.4 3.1 multiply_reduce_fusion.1
  176.4 4.9 %convolution_convert_fusion.1 = bf16[3072,768]{1,0:T(8,128)(2,1)} fusion(bf16[512,3072]{1,0:T(8,128)(2,1)S(1)} %get-tuple-element.209, f32[512,768]{1,0:T(8,128)S(1)} %get-tuple-element.150, f32[768]{0:T(1024)S(1)} %copy-done.83, f32[768]{0:T(1024)S(1)} %get-tuple-element.119, f32[512]{0:T(512)S(1)} %add_rsqrt_fusion.1, f32[512]{0:T(512)S(1)} %broadcast_multiply_fusion.5), kind=kOutput, calls=%fused_computation.34 | convolution fusion | flops 2420244480 | bytes 9447424 | tf_op jit(solution)/shard_map/dot_general | solution.py:488
  181.4 4.4 %convolution_convert_fusion = bf16[3072,768]{1,0:T(8,128)(2,1)} fusion(bf16[512,3072]{1,0:T(8,128)(2,1)S(1)} %get-tuple-element.203, f32[512,768]{1,0:T(8,128)S(1)} %get-tuple-element.142), kind=kOutput, calls=%fused_computation.33 | convolution fusion | flops 2418671616 | bytes 9437184 | tf_op jit(solution)/shard_map/dot_general | solution.py:480
  189.4 22.7 %attention_backward.1 = (bf16[2,2,2,4,104,384]{5,4,3,2,1,0:T(8,128)(2,1)S(1)}, bf16[2,2,2,4,96,384]{5,4,3,2,1,0:T(8,128)(2,1)S(1)}, f32[4,8,192]{2,1,0:T(8,128)S(1)}, f32[512,768]{1,0:T(8,128)S(1)}) custom-call(s32[8]{0:T(128)S(1)} %add.489.place_ref, bf16[512,768]{1,0:T(8,128)(2,1)S(1)} %bitcast.159, bf16[512,768]{1,0:T(8,128)(2,1)S(1)} %convert_element_type.280.gr_ref, ...), custom_call_target="tpu_custom_call" | custom-call | flops 17999998976 | bytes 16000000 | tf_op jit(solution)/shard_map/attention_backward/pallas_call | solution.py:306
  220.1 3.0 fusion.82
  229.2 8.1 %collective-permute-done.27 = bf16[2,128,768]{2,1,0:T(8,128)(2,1)S(1)} collective-permute-done((bf16[2,128,768]{2,1,0:T(8,128)(2,1)S(1)}, bf16[2,128,768]{2,1,0:T(8,128)(2,1)S(1)}, u32[]{:S(2)}, u32[]{:S(2)}) %collective-permute-start.27) | collective-permute-done | bytes 393248 | tf_op jit(solution)/shard_map/ppermute | solution.py:32
  240.7 5.0 %collective-permute-done.31 = bf16[2,128,768]{2,1,0:T(8,128)(2,1)S(1)} collective-permute-done((bf16[2,128,768]{2,1,0:T(8,128)(2,1)S(1)}, bf16[2,128,768]{2,1,0:T(8,128)(2,1)S(1)}, u32[]{:S(2)}, u32[]{:S(2)}) %collective-permute-start.31) | collective-permute-done | bytes 393248 | tf_op jit(solution)/shard_map/ppermute | solution.py:32
  245.8 11.6 %collective-permute-done.39 = bf16[1,2,1,4,96,384]{5,4,3,2,1,0:T(8,128)(2,1)S(1)} collective-permute-done((bf16[1,2,1,4,96,384]{5,4,3,2,1,0:T(8,128)(2,1)S(1)}, bf16[1,2,1,4,96,384]{5,4,3,2,1,0:T(8,128)(2,1)S(1)}, u32[]{:S(2)}, u32[]{:S(2)}) %collective-permute-start.39) | collective-permute-done | bytes 589856 | tf_op jit(solution)/shard_map/ppermute | solution.py:32
  262.5 5.1 %collective-permute-done.40 = bf16[1,1,1,4,96,384]{5,4,3,2,1,0:T(8,128)(2,1)S(1)} collective-permute-done((bf16[1,1,1,4,96,384]{5,4,3,2,1,0:T(8,128)(2,1)S(1)}, bf16[1,1,1,4,96,384]{5,4,3,2,1,0:T(8,128)(2,1)S(1)}, u32[]{:S(2)}, u32[]{:S(2)}) %collective-permute-start.40) | collective-permute-done | bytes 294944 | tf_op jit(solution)/shard_map/ppermute | solution.py:32
  271.5 7.9 %collective-permute-done.33 = bf16[1,1,2,4,104,384]{5,4,3,2,1,0:T(8,128)(2,1)S(1)} collective-permute-done((bf16[1,1,2,4,104,384]{5,4,3,2,1,0:T(8,128)(2,1)S(1)}, bf16[1,1,2,4,104,384]{5,4,3,2,1,0:T(8,128)(2,1)S(1)}, u32[]{:S(2)}, u32[]{:S(2)}) %collective-permute-start.33) | collective-permute-done | bytes 639008 | tf_op jit(solution)/shard_map/ppermute | solution.py:32
  279.5 3.2 collective-permute-start.41
  284.8 5.5 %collective-permute-done.34 = bf16[1,1,1,4,104,384]{5,4,3,2,1,0:T(8,128)(2,1)S(1)} collective-permute-done((bf16[1,1,1,4,104,384]{5,4,3,2,1,0:T(8,128)(2,1)S(1)}, bf16[1,1,1,4,104,384]{5,4,3,2,1,0:T(8,128)(2,1)S(1)}, u32[]{:S(2)}, u32[]{:S(2)}) %collective-permute-start.34) | collective-permute-done | bytes 319520 | tf_op jit(solution)/shard_map/ppermute | solution.py:32
  308.4 13.3 %collective-permute-done.45 = bf16[1,1,2,4,96,768]{5,4,3,2,1,0:T(8,128)(2,1)} collective-permute-done((bf16[1,1,2,4,96,768]{5,4,3,2,1,0:T(8,128)(2,1)}, bf16[1,1,2,4,96,768]{5,4,3,2,1,0:T(8,128)(2,1)}, u32[]{:S(2)}, u32[]{:S(2)}) %collective-permute-start.45) | collective-permute-done | bytes 1179680 | tf_op jit(solution)/shard_map/ppermute | solution.py:32
  325.0 3.0 collective-permute-done.51
  330.3 7.1 %collective-permute-done.46 = bf16[1,1,1,4,96,768]{5,4,3,2,1,0:T(8,128)(2,1)S(1)} collective-permute-done((bf16[1,1,1,4,96,768]{5,4,3,2,1,0:T(8,128)(2,1)S(1)}, bf16[1,1,1,4,96,768]{5,4,3,2,1,0:T(8,128)(2,1)S(1)}, u32[]{:S(2)}, u32[]{:S(2)}) %collective-permute-start.46) | collective-permute-done | bytes 589856 | tf_op jit(solution)/shard_map/ppermute | solution.py:32
  339.5 2.8 collective-permute-start.47
  348.5 3.7 %collective-permute-done.48 = bf16[1,1,1,1,96,768]{5,4,3,2,1,0:T(8,128)(2,1)S(1)} collective-permute-done((bf16[1,1,1,1,96,768]{5,4,3,2,1,0:T(8,128)(2,1)S(1)}, bf16[1,1,1,1,96,768]{5,4,3,2,1,0:T(8,128)(2,1)S(1)}, u32[]{:S(2)}, u32[]{:S(2)}) %collective-permute-start.48) | collective-permute-done | bytes 147488 | tf_op jit(solution)/shard_map/ppermute | solution.py:32
  355.0 6.6 %collective-permute-done.54 = bf16[1,1,1,1,96,768]{5,4,3,2,1,0:T(8,128)(2,1)S(1)} collective-permute-done((bf16[1,1,1,1,96,768]{5,4,3,2,1,0:T(8,128)(2,1)S(1)}, bf16[1,1,1,1,96,768]{5,4,3,2,1,0:T(8,128)(2,1)S(1)}, u32[]{:S(2)}, u32[]{:S(2)}) %collective-permute-start.54) | collective-permute-done | bytes 147488 | tf_op jit(solution)/shard_map/ppermute | solution.py:32
  (470 shorter events, 154.2 us)
Async XLA Ops:
  1.7 23.0 %collective-permute-start.16 = (bf16[1,1,1,1,96,768]{5,4,3,2,1,0:T(8,128)(2,1)S(1)}, bf16[1,1,1,1,96,768]{5,4,3,2,1,0:T(8,128)(2,1)S(1)}, u32[]{:S(2)}, u32[]{:S(2)}) collective-permute-start(bf16[1,1,1,1,96,768]{5,4,3,2,1,0:T(8,128)(2,1)S(1)} %convert_bitcast_fusion.1), channel_id=1, source_target_pairs={{0,24},{8,0},{16,8},{24,16},{1,25},{9,1},{17,9},{25,17},{2,26},{10... | collective-permute-start | bytes 442376 | tf_op jit(solution)/shard_map/ppermute | solution.py:32
  6.8 17.9 %collective-permute-start.15 = (bf16[1,1,1,1,96,768]{5,4,3,2,1,0:T(8,128)(2,1)S(1)}, bf16[1,1,1,1,96,768]{5,4,3,2,1,0:T(8,128)(2,1)S(1)}, u32[]{:S(2)}, u32[]{:S(2)}) collective-permute-start(bf16[1,1,1,1,96,768]{5,4,3,2,1,0:T(8,128)(2,1)S(1)} %convert_bitcast_fusion.1), channel_id=1, source_target_pairs={{0,16},{8,24},{16,0},{24,8},{1,17},{9,25},{17,1},{25,9},{2,18},{10... | collective-permute-start | bytes 442376 | tf_op jit(solution)/shard_map/ppermute | solution.py:32
  6.8 21.7 %collective-permute-start.14 = (bf16[1,1,1,1,96,768]{5,4,3,2,1,0:T(8,128)(2,1)S(1)}, bf16[1,1,1,1,96,768]{5,4,3,2,1,0:T(8,128)(2,1)S(1)}, u32[]{:S(2)}, u32[]{:S(2)}) collective-permute-start(bf16[1,1,1,1,96,768]{5,4,3,2,1,0:T(8,128)(2,1)S(1)} %convert_bitcast_fusion.1), channel_id=1, source_target_pairs={{0,8},{8,16},{16,24},{24,0},{1,9},{9,17},{17,25},{25,1},{2,10},{10... | collective-permute-start | bytes 442376 | tf_op jit(solution)/shard_map/ppermute | solution.py:32
  10.6 18.0 %collective-permute-start.10 = (bf16[1,1,1,1,96,384]{5,4,3,2,1,0:T(8,128)(2,1)}, bf16[1,1,1,1,96,384]{5,4,3,2,1,0:T(8,128)(2,1)S(1)}, u32[]{:S(2)}, u32[]{:S(2)}) collective-permute-start(bf16[1,1,1,1,96,384]{5,4,3,2,1,0:T(8,128)(2,1)} %pad_maximum_fusion.23), channel_id=1, source_target_pairs={{0,24},{8,0},{16,8},{24,16},{1,25},{9,1},{17,9},{25,17},{2,26},{10... | collective-permute-start | bytes 221192 | tf_op jit(solution)/shard_map/ppermute | solution.py:32
  13.4 15.9 %collective-permute-start.9 = (bf16[1,1,1,1,96,384]{5,4,3,2,1,0:T(8,128)(2,1)}, bf16[1,1,1,1,96,384]{5,4,3,2,1,0:T(8,128)(2,1)S(1)}, u32[]{:S(2)}, u32[]{:S(2)}) collective-permute-start(bf16[1,1,1,1,96,384]{5,4,3,2,1,0:T(8,128)(2,1)} %pad_maximum_fusion.23), channel_id=1, source_target_pairs={{0,16},{8,24},{16,0},{24,8},{1,17},{9,25},{17,1},{25,9},{2,18},{10... | collective-permute-start | bytes 221192 | tf_op jit(solution)/shard_map/ppermute | solution.py:32
  29.4 25.6 %collective-permute-start.17 = (bf16[1,1,1,4,96,768]{5,4,3,2,1,0:T(8,128)(2,1)S(1)}, bf16[1,1,1,4,96,768]{5,4,3,2,1,0:T(8,128)(2,1)S(1)}, u32[]{:S(2)}, u32[]{:S(2)}) collective-permute-start(bf16[1,1,1,4,96,768]{5,4,3,2,1,0:T(8,128)(2,1)S(1)} %pad_maximum_fusion.16), channel_id=1, source_target_pairs={{0,2},{2,0},{1,3},{3,1},{4,6},{6,4},{5,7},{7,5},{8,10},{10,8},{9,1... | collective-permute-start | bytes 1769480 | tf_op jit(solution)/shard_map/ppermute | solution.py:32
  32.1 20.5 %collective-permute-start.11 = (bf16[1,1,1,4,96,384]{5,4,3,2,1,0:T(8,128)(2,1)S(1)}, bf16[1,1,1,4,96,384]{5,4,3,2,1,0:T(8,128)(2,1)S(1)}, u32[]{:S(2)}, u32[]{:S(2)}) collective-permute-start(bf16[1,1,1,4,96,384]{5,4,3,2,1,0:T(8,128)(2,1)S(1)} %pad_maximum_fusion.21), channel_id=1, source_target_pairs={{0,4},{4,0},{1,5},{5,1},{2,6},{6,2},{3,7},{7,3},{8,12},{12,8},{9,1... | collective-permute-start | bytes 884744 | tf_op jit(solution)/shard_map/ppermute | solution.py:32
  45.5 25.2 %collective-permute-start = (bf16[2,128,768]{2,1,0:T(8,128)(2,1)}, bf16[2,128,768]{2,1,0:T(8,128)(2,1)}, u32[]{:S(2)}, u32[]{:S(2)}) collective-permute-start(bf16[2,128,768]{2,1,0:T(8,128)(2,1)} %bitcast.154), channel_id=1, source_target_pairs={{0,2},{2,0},{1,3},{3,1},{4,6},{6,4},{5,7},{7,5},{8,10},{10,8},{9,1... | collective-permute-start | bytes 1179656 | tf_op jit(solution)/shard_map/ppermute | solution.py:32
  48.8 20.8 %collective-permute-start.23 = (bf16[1,1,1,4,96,768]{5,4,3,2,1,0:T(8,128)(2,1)}, bf16[1,1,1,4,96,768]{5,4,3,2,1,0:T(8,128)(2,1)S(1)}, u32[]{:S(2)}, u32[]{:S(2)}) collective-permute-start(bf16[1,1,1,4,96,768]{5,4,3,2,1,0:T(8,128)(2,1)} %pad_maximum_fusion.17), channel_id=1, source_target_pairs={{0,4},{4,0},{1,5},{5,1},{2,6},{6,2},{3,7},{7,3},{8,12},{12,8},{9,1... | collective-permute-start | bytes 1769480 | tf_op jit(solution)/shard_map/ppermute | solution.py:32
  51.1 15.7 %collective-permute-start.5 = (bf16[1,1,1,4,97,384]{5,4,3,2,1,0:T(8,128)(2,1)}, bf16[1,1,1,4,97,384]{5,4,3,2,1,0:T(8,128)(2,1)S(1)}, u32[]{:S(2)}, u32[]{:S(2)}) collective-permute-start(bf16[1,1,1,4,97,384]{5,4,3,2,1,0:T(8,128)(2,1)} %pad_maximum_fusion.20), channel_id=1, source_target_pairs={{0,2},{2,0},{1,3},{3,1},{4,6},{6,4},{5,7},{7,5},{8,10},{10,8},{9,1... | collective-permute-start | bytes 893960 | tf_op jit(solution)/shard_map/ppermute | solution.py:32
  54.4 21.9 %collective-permute-start.12 = (bf16[1,2,1,4,96,384]{5,4,3,2,1,0:T(8,128)(2,1)}, bf16[1,2,1,4,96,384]{5,4,3,2,1,0:T(8,128)(2,1)}, u32[]{:S(2)}, u32[]{:S(2)}) collective-permute-start(bf16[1,2,1,4,96,384]{5,4,3,2,1,0:T(8,128)(2,1)} %pad_maximum_fusion.15), channel_id=1, source_target_pairs={{0,2},{2,0},{1,3},{3,1},{4,6},{6,4},{5,7},{7,5},{8,10},{10,8},{9,1... | collective-permute-start | bytes 1769480 | tf_op jit(solution)/shard_map/ppermute | solution.py:32
  56.2 43.9 %collective-permute-start.18 = (bf16[1,1,2,4,96,768]{5,4,3,2,1,0:T(8,128)(2,1)}, bf16[1,1,2,4,96,768]{5,4,3,2,1,0:T(8,128)(2,1)}, u32[]{:S(2)}, u32[]{:S(2)}) collective-permute-start(bf16[1,1,2,4,96,768]{5,4,3,2,1,0:T(8,128)(2,1)} %pad_maximum_fusion.8), channel_id=1, source_target_pairs={{0,4},{4,0},{1,5},{5,1},{2,6},{6,2},{3,7},{7,3},{8,12},{12,8},{9,1... | collective-permute-start | bytes 3538952 | tf_op jit(solution)/shard_map/ppermute | solution.py:32
  66.8 17.9 %collective-permute-start.28 = (bf16[2,128,768]{2,1,0:T(8,128)(2,1)}, bf16[2,128,768]{2,1,0:T(8,128)(2,1)S(1)}, u32[]{:S(2)}, u32[]{:S(2)}) collective-permute-start(bf16[2,128,768]{2,1,0:T(8,128)(2,1)} %bitcast.152), channel_id=1, source_target_pairs={{0,2},{2,0},{1,3},{3,1},{4,6},{6,4},{5,7},{7,5},{8,10},{10,8},{9,1... | collective-permute-start | bytes 1179656 | tf_op jit(solution)/shard_map/ppermute | solution.py:32
  69.6 29.0 %collective-permute-start.6 = (bf16[1,1,2,4,97,384]{5,3,4,2,1,0:T(4,128)(2,1)S(1)}, bf16[1,1,2,4,97,384]{5,3,4,2,1,0:T(4,128)(2,1)S(1)}, u32[]{:S(2)}, u32[]{:S(2)}) collective-permute-start(bf16[1,1,2,4,97,384]{5,3,4,2,1,0:T(4,128)(2,1)S(1)} %copy.77), channel_id=1, source_target_pairs={{0,4},{4,0},{1,5},{5,1},{2,6},{6,2},{3,7},{7,3},{8,12},{12,8},{9,1... | collective-permute-start | bytes 1787912 | tf_op jit(solution)/shard_map/ppermute | solution.py:32
  70.7 35.9 %collective-permute-start.24 = (bf16[1,2,1,4,96,768]{5,4,3,2,1,0:T(8,128)(2,1)S(1)}, bf16[1,2,1,4,96,768]{5,4,3,2,1,0:T(8,128)(2,1)S(1)}, u32[]{:S(2)}, u32[]{:S(2)}) collective-permute-start(bf16[1,2,1,4,96,768]{5,4,3,2,1,0:T(8,128)(2,1)S(1)} %pad_maximum_fusion.9), channel_id=1, source_target_pairs={{0,2},{2,0},{1,3},{3,1},{4,6},{6,4},{5,7},{7,5},{8,10},{10,8},{9,1... | collective-permute-start | bytes 3538952 | tf_op jit(solution)/shard_map/ppermute | solution.py:32
  76.3 23.1 %collective-permute-start.1 = (bf16[2,128,768]{2,1,0:T(8,128)(2,1)S(1)}, bf16[2,128,768]{2,1,0:T(8,128)(2,1)S(1)}, u32[]{:S(2)}, u32[]{:S(2)}) collective-permute-start(bf16[2,128,768]{2,1,0:T(8,128)(2,1)S(1)} %get-tuple-element.175), channel_id=1, source_target_pairs={{0,1},{1,0},{2,3},{3,2},{4,5},{5,4},{6,7},{7,6},{8,9},{9,8},{10,11... | collective-permute-start | bytes 1179656 | tf_op jit(solution)/shard_map/ppermute | solution.py:32
  84.6 23.8 %collective-permute-start.13 = (bf16[1,2,2,4,96,384]{5,4,3,2,1,0:T(8,128)(2,1)S(1)}, bf16[1,2,2,4,96,384]{5,4,3,2,1,0:T(8,128)(2,1)S(1)}, u32[]{:S(2)}, u32[]{:S(2)}) collective-permute-start(bf16[1,2,2,4,96,384]{5,4,3,2,1,0:T(8,128)(2,1)S(1)} %pad_maximum_fusion.7), channel_id=1, source_target_pairs={{0,1},{1,0},{2,3},{3,2},{4,5},{5,4},{6,7},{7,6},{8,9},{9,8},{10,11... | collective-permute-start | bytes 3538952 | tf_op jit(solution)/shard_map/ppermute | solution.py:32
  98.6 40.2 %collective-permute-start.29 = (bf16[2,128,768]{2,1,0:T(8,128)(2,1)}, bf16[2,128,768]{2,1,0:T(8,128)(2,1)}, u32[]{:S(2)}, u32[]{:S(2)}) collective-permute-start(bf16[2,128,768]{2,1,0:T(8,128)(2,1)} %get-tuple-element.167), channel_id=1, source_target_pairs={{0,1},{1,0},{2,3},{3,2},{4,5},{5,4},{6,7},{7,6},{8,9},{9,8},{10,11... | collective-permute-start | bytes 1179656 | tf_op jit(solution)/shard_map/ppermute | solution.py:32
  103.0 37.2 %collective-permute-start.19 = (bf16[1,2,2,4,96,768]{5,4,3,2,1,0:T(8,128)(2,1)}, bf16[1,2,2,4,96,768]{5,4,3,2,1,0:T(8,128)(2,1)}, u32[]{:S(2)}, u32[]{:S(2)}) collective-permute-start(bf16[1,2,2,4,96,768]{5,4,3,2,1,0:T(8,128)(2,1)} %pad_maximum_fusion.4), channel_id=1, source_target_pairs={{0,1},{1,0},{2,3},{3,2},{4,5},{5,4},{6,7},{7,6},{8,9},{9,8},{10,11... | collective-permute-start | bytes 7077896 | tf_op jit(solution)/shard_map/ppermute | solution.py:32
  108.5 50.9 %collective-permute-start.25 = (bf16[1,2,2,4,96,768]{5,4,3,2,1,0:T(8,128)(2,1)}, bf16[1,2,2,4,96,768]{5,4,3,2,1,0:T(8,128)(2,1)}, u32[]{:S(2)}, u32[]{:S(2)}) collective-permute-start(bf16[1,2,2,4,96,768]{5,4,3,2,1,0:T(8,128)(2,1)} %pad_maximum_fusion.5), channel_id=1, source_target_pairs={{0,1},{1,0},{2,3},{3,2},{4,5},{5,4},{6,7},{7,6},{8,9},{9,8},{10,11... | collective-permute-start | bytes 7077896 | tf_op jit(solution)/shard_map/ppermute | solution.py:32
  186.7 36.9 %collective-permute-start.26 = (bf16[2,128,768]{2,1,0:T(8,128)(2,1)}, bf16[2,128,768]{2,1,0:T(8,128)(2,1)}, u32[]{:S(2)}, u32[]{:S(2)}) collective-permute-start(bf16[2,128,768]{2,1,0:T(8,128)(2,1)} %bitcast.21), channel_id=1, source_target_pairs={{0,1},{1,0},{2,3},{3,2},{4,5},{5,4},{6,7},{7,6},{8,9},{9,8},{10,11... | collective-permute-start | bytes 1179656 | tf_op jit(solution)/shard_map/ppermute | solution.py:32
  219.5 39.9 %collective-permute-start.32 = (bf16[1,2,2,4,104,384]{5,4,3,2,1,0:T(8,128)(2,1)S(1)}, bf16[1,2,2,4,104,384]{5,4,3,2,1,0:T(8,128)(2,1)S(1)}, u32[]{:S(2)}, u32[]{:S(2)}) collective-permute-start(bf16[1,2,2,4,104,384]{5,4,3,2,1,0:T(8,128)(2,1)S(1)} %slice.331), channel_id=1, source_target_pairs={{0,1},{1,0},{2,3},{3,2},{4,5},{5,4},{6,7},{7,6},{8,9},{9,8},{10,11... | collective-permute-start | bytes 3833864 | tf_op jit(solution)/shard_map/ppermute | solution.py:32
  223.1 71.9 %collective-permute-start.44 = (bf16[1,2,2,4,96,768]{5,4,3,2,1,0:T(8,128)(2,1)S(1)}, bf16[1,2,2,4,96,768]{5,4,3,2,1,0:T(8,128)(2,1)S(1)}, u32[]{:S(2)}, u32[]{:S(2)}) collective-permute-start(bf16[1,2,2,4,96,768]{5,4,3,2,1,0:T(8,128)(2,1)S(1)} %bitcast.170), channel_id=1, source_target_pairs={{0,1},{1,0},{2,3},{3,2},{4,5},{5,4},{6,7},{7,6},{8,9},{9,8},{10,11... | collective-permute-start | bytes 7077896 | tf_op jit(solution)/shard_map/ppermute | solution.py:32
  223.5 75.0 %collective-permute-start.50 = (bf16[1,2,2,4,96,768]{5,4,3,2,1,0:T(8,128)(2,1)S(1)}, bf16[1,2,2,4,96,768]{5,4,3,2,1,0:T(8,128)(2,1)S(1)}, u32[]{:S(2)}, u32[]{:S(2)}) collective-permute-start(bf16[1,2,2,4,96,768]{5,4,3,2,1,0:T(8,128)(2,1)S(1)} %bitcast.169), channel_id=1, source_target_pairs={{0,1},{1,0},{2,3},{3,2},{4,5},{5,4},{6,7},{7,6},{8,9},{9,8},{10,11... | collective-permute-start | bytes 7077896 | tf_op jit(solution)/shard_map/ppermute | solution.py:32
  227.2 18.5 %collective-permute-start.31 = (bf16[2,128,768]{2,1,0:T(8,128)(2,1)S(1)}, bf16[2,128,768]{2,1,0:T(8,128)(2,1)S(1)}, u32[]{:S(2)}, u32[]{:S(2)}) collective-permute-start(bf16[2,128,768]{2,1,0:T(8,128)(2,1)S(1)} %fusion.36), channel_id=1, source_target_pairs={{0,2},{2,0},{1,3},{3,1},{4,6},{6,4},{5,7},{7,5},{8,10},{10,8},{9,1... | collective-permute-start | bytes 1179656 | tf_op jit(solution)/shard_map/ppermute | solution.py:32
  237.3 20.1 %collective-permute-start.39 = (bf16[1,2,1,4,96,384]{5,4,3,2,1,0:T(8,128)(2,1)S(1)}, bf16[1,2,1,4,96,384]{5,4,3,2,1,0:T(8,128)(2,1)S(1)}, u32[]{:S(2)}, u32[]{:S(2)}) collective-permute-start(bf16[1,2,1,4,96,384]{5,4,3,2,1,0:T(8,128)(2,1)S(1)} %slice.343), channel_id=1, source_target_pairs={{0,2},{2,0},{1,3},{3,1},{4,6},{6,4},{5,7},{7,5},{8,10},{10,8},{9,1... | collective-permute-start | bytes 1769480 | tf_op jit(solution)/shard_map/ppermute | solution.py:32
  259.8 19.7 %collective-permute-start.33 = (bf16[1,1,2,4,104,384]{5,4,3,2,1,0:T(8,128)(2,1)S(1)}, bf16[1,1,2,4,104,384]{5,4,3,2,1,0:T(8,128)(2,1)S(1)}, u32[]{:S(2)}, u32[]{:S(2)}) collective-permute-start(bf16[1,1,2,4,104,384]{5,4,3,2,1,0:T(8,128)(2,1)S(1)} %slice.333), channel_id=1, source_target_pairs={{0,4},{4,0},{1,5},{5,1},{2,6},{6,2},{3,7},{7,3},{8,12},{12,8},{9,1... | collective-permute-start | bytes 1916936 | tf_op jit(solution)/shard_map/ppermute | solution.py:32
  267.7 15.1 %collective-permute-start.43 = (bf16[1,1,1,1,96,384]{5,4,3,2,1,0:T(8,128)(2,1)S(1)}, bf16[1,1,1,1,96,384]{5,4,3,2,1,0:T(8,128)(2,1)S(1)}, u32[]{:S(2)}, u32[]{:S(2)}) collective-permute-start(bf16[1,1,1,1,96,384]{5,4,3,2,1,0:T(8,128)(2,1)S(1)} %get-tuple-element.188), channel_id=1, source_target_pairs={{0,8},{8,16},{16,24},{24,0},{1,9},{9,17},{17,25},{25,1},{2,10},{10... | collective-permute-start | bytes 221192 | tf_op jit(solution)/shard_map/ppermute | solution.py:32
  297.0 24.7 %collective-permute-start.45 = (bf16[1,1,2,4,96,768]{5,4,3,2,1,0:T(8,128)(2,1)}, bf16[1,1,2,4,96,768]{5,4,3,2,1,0:T(8,128)(2,1)}, u32[]{:S(2)}, u32[]{:S(2)}) collective-permute-start(bf16[1,1,2,4,96,768]{5,4,3,2,1,0:T(8,128)(2,1)} %slice.355), channel_id=1, source_target_pairs={{0,4},{4,0},{1,5},{5,1},{2,6},{6,2},{3,7},{7,3},{8,12},{12,8},{9,1... | collective-permute-start | bytes 3538952 | tf_op jit(solution)/shard_map/ppermute | solution.py:32
  300.4 27.5 %collective-permute-start.51 = (bf16[1,2,1,4,96,768]{5,4,3,2,1,0:T(8,128)(2,1)}, bf16[1,2,1,4,96,768]{5,4,3,2,1,0:T(8,128)(2,1)}, u32[]{:S(2)}, u32[]{:S(2)}) collective-permute-start(bf16[1,2,1,4,96,768]{5,4,3,2,1,0:T(8,128)(2,1)} %slice.365), channel_id=1, source_target_pairs={{0,2},{2,0},{1,3},{3,1},{4,6},{6,4},{5,7},{7,5},{8,10},{10,8},{9,1... | collective-permute-start | bytes 3538952 | tf_op jit(solution)/shard_map/ppermute | solution.py:32
  342.6 19.1 %collective-permute-start.54 = (bf16[1,1,1,1,96,768]{5,4,3,2,1,0:T(8,128)(2,1)S(1)}, bf16[1,1,1,1,96,768]{5,4,3,2,1,0:T(8,128)(2,1)S(1)}, u32[]{:S(2)}, u32[]{:S(2)}) collective-permute-start(bf16[1,1,1,1,96,768]{5,4,3,2,1,0:T(8,128)(2,1)S(1)} %get-tuple-element.180), channel_id=1, source_target_pairs={{0,16},{8,24},{16,0},{24,8},{1,17},{9,25},{17,1},{25,9},{2,18},{10... | collective-permute-start | bytes 442376 | tf_op jit(solution)/shard_map/ppermute | solution.py:32
  346.4 15.3 %collective-permute-start.53 = (bf16[1,1,1,1,96,768]{5,4,3,2,1,0:T(8,128)(2,1)S(1)}, bf16[1,1,1,1,96,768]{5,4,3,2,1,0:T(8,128)(2,1)S(1)}, u32[]{:S(2)}, u32[]{:S(2)}) collective-permute-start(bf16[1,1,1,1,96,768]{5,4,3,2,1,0:T(8,128)(2,1)S(1)} %get-tuple-element.178), channel_id=1, source_target_pairs={{0,24},{8,0},{16,8},{24,16},{1,25},{9,1},{17,9},{25,17},{2,26},{10... | collective-permute-start | bytes 442376 | tf_op jit(solution)/shard_map/ppermute | solution.py:32
  (115 other events, 1686.7 us)
